TPU v7x, 512 devices: a whole 4x8x8 slice. The times are simulated.
512 devices in a mesh: gx: 64 (over z, x, core), gy: 8 (over y).
Axes of the slice: x: 4, y: 8, z: 8, core: 2. Of those that a mesh axis runs over, the one named last changes fastest.
Arguments:
- field: bfloat16 [16, 256, 192, 512], P(None, 'gx', 'gy'), may hold values from -6 to 6
- pointwise: bfloat16 [16, 16], replicated, may hold values from -1.5 to 1.5
- spectral: float32 [2304, 2, 16, 16, 32], P('gx', None, None, None, 'gy'), may hold values from -1 to 1
- momentum: float32 [2304, 2, 16, 16, 32], P('gx', None, None, None, 'gy'), may hold values from -6 to 6
- cotangent: bfloat16 [16, 256, 192, 512], P(None, 'gx', 'gy'), may hold values from -6 to 6
Outputs:
- momentum_next: float32 [2304, 2, 16, 16, 32], P('gx', None, None, None, 'gy')
All inputs are finite; a program needn't handle non-finite values.
Results may differ from a plain program's by a relative error of at most 0.0025.
Values may be sent and summed in bfloat16 or wider, within the bound.
No kernel may reach another device: no remote copies, remote signals or barrier semaphores. Data moves between devices by JAX's collectives and lax.ppermute only.
A program may use at most 64 MiB of HBM per device.

v0:
```python
import math

import jax
import jax.numpy as jnp
from jax import lax
from jax.sharding import PartitionSpec as P

C = 16
MX = 48
MY = 48
MZ = 32


HIGH = lax.Precision.HIGHEST


def phase(first, second, length):
    return 2.0 * math.pi / length * (first * second % length).astype(jnp.float32)


def gelu_slope(pre):
    inner = 0.7978845608 * (pre + 0.044715 * pre * pre * pre)
    tanh_inner = jnp.tanh(inner)
    return 0.5 * (1.0 + tanh_inner) + 0.5 * pre * (1.0 - tanh_inner * tanh_inner) * 0.7978845608 * (
        1.0 + 3.0 * 0.044715 * pre * pre
    )


def z_forward(field):
    depth = field.shape[-1]
    zpos = lax.broadcasted_iota(jnp.int32, (depth, MZ), 0)
    kpos = lax.broadcasted_iota(jnp.int32, (depth, MZ), 1)
    angle = phase(zpos, kpos, depth)
    table = jnp.concatenate([jnp.cos(angle), -jnp.sin(angle)], axis=1).astype(jnp.bfloat16)
    flat = jnp.dot(field.reshape(-1, depth), table, preferred_element_type=jnp.float32)
    scaled = (flat / math.sqrt(depth)).astype(jnp.bfloat16)
    return scaled.reshape(field.shape[:-1] + (2, MZ))


def y_forward(zmodes, ypos, total_y):
    kvals = lax.broadcasted_iota(jnp.int32, (ypos.shape[0], MY), 1)
    angle = phase(ypos[:, None], kvals, total_y)
    cos_t = jnp.cos(angle) / math.sqrt(total_y)
    sin_t = jnp.sin(angle) / math.sqrt(total_y)
    real_in = zmodes[:, :, :, 0, :].astype(jnp.float32)
    imag_in = zmodes[:, :, :, 1, :].astype(jnp.float32)
    form = "cxyk,yq->xqck"
    real_out = jnp.einsum(form, real_in, cos_t, precision=HIGH) + jnp.einsum(
        form, imag_in, sin_t, precision=HIGH
    )
    imag_out = jnp.einsum(form, imag_in, cos_t, precision=HIGH) - jnp.einsum(
        form, real_in, sin_t, precision=HIGH
    )
    return (real_out, imag_out)


def forward_x(values, kxs, xpos, total_x):
    angle = phase(kxs, xpos, total_x)
    cos_t = jnp.cos(angle) / math.sqrt(total_x)
    sin_t = jnp.sin(angle) / math.sqrt(total_x)
    real_in = values[:, :, 0]
    imag_in = values[:, :, 1]
    form = "px,xqn->pqn"
    real_out = jnp.einsum(form, cos_t, real_in, precision=HIGH) + jnp.einsum(
        form, sin_t, imag_in, precision=HIGH
    )
    imag_out = jnp.einsum(form, cos_t, imag_in, precision=HIGH) - jnp.einsum(
        form, sin_t, real_in, precision=HIGH
    )
    return jnp.stack([real_out, imag_out], 2)


def inverse_x(values, kxs, xpos, total_x):
    angle = phase(kxs, xpos, total_x)
    cos_t = jnp.cos(angle)
    sin_t = jnp.sin(angle)
    real_in = values[:, :, 0]
    imag_in = values[:, :, 1]
    form = "px,pqn->xqn"
    real_out = jnp.einsum(form, cos_t, real_in, precision=HIGH) - jnp.einsum(
        form, sin_t, imag_in, precision=HIGH
    )
    imag_out = jnp.einsum(form, sin_t, real_in, precision=HIGH) + jnp.einsum(
        form, cos_t, imag_in, precision=HIGH
    )
    return jnp.stack([real_out, imag_out], 2)


def x_modes(ycoef, total_x):
    rows_x = ycoef.shape[0]
    width = ycoef.shape[3]
    offset = lax.axis_index("gx") * rows_x
    kxs = lax.broadcasted_iota(jnp.int32, (MX, rows_x), 0)
    xpos = offset + lax.broadcasted_iota(jnp.int32, (MX, rows_x), 1)
    flat = forward_x(ycoef, kxs, xpos, total_x).reshape(MX * MY, 2 * width)
    spectrum = lax.psum_scatter(flat, "gx", scatter_dimension=0, tiled=True)
    return spectrum.reshape(-1, 2, width)


def to_owners(field):
    rows_x = field.shape[1]
    rows_y = field.shape[2]
    zmodes = z_forward(field)
    total_y = rows_y * lax.axis_size("gy")
    ypos = lax.axis_index("gy") * rows_y + lax.broadcasted_iota(jnp.int32, (rows_y,), 0)
    real_out, imag_out = y_forward(zmodes, ypos, total_y)
    summed = lax.psum_scatter(
        jnp.transpose(jnp.stack([real_out, imag_out], 2), (4, 0, 1, 2, 3)).astype(jnp.bfloat16),
        "gy",
        scatter_dimension=0,
        tiled=True,
    ).astype(jnp.float32)
    ycoef = jnp.transpose(summed, (1, 2, 3, 4, 0))
    local_z = ycoef.shape[4]
    ycoef = ycoef.reshape(rows_x, MY, 2, C * local_z)
    spectrum = x_modes(ycoef, rows_x * lax.axis_size("gx"))
    return spectrum.reshape(-1, 2, C, local_z)


def on_device(field, pointwise, spectral, momentum, cotangent):
    rows_x = field.shape[1]
    rows_y = field.shape[2]
    spectrum = to_owners(field)
    real_f = spectrum[:, 0]
    imag_f = spectrum[:, 1]
    real_w = spectral[:, 0]
    imag_w = spectral[:, 1]
    form = "qcok,qck->qok"
    mixed_r = jnp.einsum(form, real_w, real_f, precision=HIGH) - jnp.einsum(
        form, imag_w, imag_f, precision=HIGH
    )
    mixed_i = jnp.einsum(form, real_w, imag_f, precision=HIGH) + jnp.einsum(
        form, imag_w, real_f, precision=HIGH
    )
    mixed = jnp.stack([mixed_r, mixed_i], 1).astype(jnp.bfloat16)
    owned = mixed.shape[0]
    local_z = mixed.shape[3]
    columns_all = C * local_z
    flat_mixed = mixed.reshape(owned, 2, columns_all)
    total_x = rows_x * lax.axis_size("gx")
    gathered = lax.all_gather(flat_mixed, "gx", axis=0, tiled=True)
    offset = lax.axis_index("gx") * rows_x
    kxs = lax.broadcasted_iota(jnp.int32, (MX, rows_x), 0)
    xpos = offset + lax.broadcasted_iota(jnp.int32, (MX, rows_x), 1)
    back = inverse_x(
        gathered.astype(jnp.float32).reshape(MX, MY, 2, columns_all), kxs, xpos, total_x
    )
    back_r = back[:, :, 0].reshape(rows_x, MY, C, local_z)
    back_i = back[:, :, 1].reshape(rows_x, MY, C, local_z)
    total_y = rows_y * lax.axis_size("gy")
    kys = lax.broadcasted_iota(jnp.int32, (MY, total_y), 0)
    ypos = lax.broadcasted_iota(jnp.int32, (MY, total_y), 1)
    angle_y = phase(kys, ypos, total_y)
    factor = 1.0 / math.sqrt(MX * MY * MZ)
    cos_y = jnp.cos(angle_y) * factor
    sin_y = jnp.sin(angle_y) * factor
    form = "xqck,qy->xyck"
    wave_r = jnp.einsum(form, back_r, cos_y, precision=HIGH) - jnp.einsum(
        form, back_i, sin_y, precision=HIGH
    )
    wave_i = jnp.einsum(form, back_r, sin_y, precision=HIGH) + jnp.einsum(
        form, back_i, cos_y, precision=HIGH
    )
    waves = jnp.stack([wave_r, wave_i], 2).astype(jnp.bfloat16)
    waves = lax.all_to_all(waves, "gy", split_axis=1, concat_axis=4, tiled=True)
    depth = field.shape[3]
    kzs = lax.broadcasted_iota(jnp.int32, (MZ, depth), 0)
    zpos = lax.broadcasted_iota(jnp.int32, (MZ, depth), 1)
    angle_z = phase(kzs, zpos, depth)
    ztable = jnp.stack([jnp.cos(angle_z), -jnp.sin(angle_z)], 0).astype(jnp.bfloat16)
    spec_out = jnp.einsum("xyrck,rkz->cxyz", waves, ztable, preferred_element_type=jnp.float32)
    pre = spec_out + jnp.einsum(
        "co,cxyz->oxyz", pointwise, field, preferred_element_type=jnp.float32
    )
    grad_pre = (cotangent.astype(jnp.float32) * gelu_slope(pre)).astype(jnp.bfloat16)
    grads = to_owners(grad_pre)
    grad_r = grads[:, 0]
    grad_i = grads[:, 1]
    d_real = grad_r[:, None] * real_f[:, :, None] + grad_i[:, None] * imag_f[:, :, None]
    d_imag = grad_i[:, None] * real_f[:, :, None] - grad_r[:, None] * imag_f[:, :, None]
    total = jnp.stack([d_real, d_imag], 1) + 2.0 * C * spectral
    return momentum - 0.25 * total


def solution(mesh):
    in_specs = (
        P(None, "gx", "gy", None),
        P(),
        P("gx", None, None, None, "gy"),
        P("gx", None, None, None, "gy"),
        P(None, "gx", "gy", None),
    )
    out_specs = P("gx", None, None, None, "gy")
    return jax.shard_map(
        on_device, mesh=mesh, in_specs=in_specs, out_specs=out_specs, check_vma=False
    )
```

profile of v0, /device:TPU:1, one launch (start us, length us, event | category | flops | bytes accessed | tf_op | source)
XLA Modules:
  0.0 627.4 jit_solution(3908451148046801691)
XLA Ops:
  8.6 1.7 reshape.149
  10.3 1.4 fusion.314
  11.7 1.6 copy.194
  17.2 1.6 copy.123
  19.1 42.1 %reduce-scatter.3.cloned.1.call-done = bf16[4,4,48,2,16]{2,4,3,1,0:T(8,128)(2,1)} async-done(((bf16[32,4,48,2,16]{2,4,3,1,0:T(8,128)(2,1)}), bf16[4,4,48,2,16]{2,4,3,1,0:T(8,128)(2,1)}) %reduce-scatter.3.cloned.1.call-update) | async-done | bytes 49168 | tf_op jit(solution)/shard_map/reduce_scatter | solution.py:107
  66.0 3.2 copy.127
  69.2 3.5 reshape.122
  74.8 198.0 %all-reduce.5.cloned.1.call-done = f32[2304,128]{1,0:T(8,128)} async-done(((f32[2304,128]{1,0:T(8,128)}), f32[2304,128]{1,0:T(8,128)}) %all-reduce.5.cloned.1.call-update) | async-done | bytes 1179664
  275.0 51.3 %all_gather.3 = bf16[2304,2,64]{2,1,0:T(2,128)(2,1)S(1)} all-gather(bf16[36,2,64]{2,1,0:T(2,128)(2,1)S(1)} %copy.129), channel_id=1, replica_groups=mesh['gx'=64,'gy'=8] {'gx'}, dimensions={0}, use_global_device_ids=true | all-gather | bytes 599040 | tf_op jit(solution)/shard_map/all_gather | solution.py:141
  326.3 1.6 fusion.312
  334.5 2.3 reshape.151
  336.7 6.5 %all-to-all-start = ((bf16[8,2,6144]{2,1,0:T(2,128)(2,1)}), bf16[8,2,6144]{2,1,0:T(2,128)(2,1)S(1)}, u32[]{:S(2)}, u32[]{:S(2)}) async-start(bf16[8,2,6144]{2,1,0:T(2,128)(2,1)} %reshape.151), calls=%async_computation.1 | async-start | bytes 393216 | tf_op jit(solution)/shard_map/all_to_all | solution.py:165
  343.7 2.7 fusion.10
  346.4 6.7 %all-to-all-done = bf16[8,2,6144]{2,1,0:T(2,128)(2,1)S(1)} async-done(((bf16[8,2,6144]{2,1,0:T(2,128)(2,1)}), bf16[8,2,6144]{2,1,0:T(2,128)(2,1)S(1)}, u32[]{:S(2)}, u32[]{:S(2)}) %all-to-all-start) | async-done | bytes 196640 | tf_op jit(solution)/shard_map/all_to_all | solution.py:165
  354.2 3.3 copy.140
  357.5 5.5 fusion.6
  364.4 1.7 reshape.150
  367.5 1.6 copy.200
  373.0 1.6 copy.149
  374.9 30.3 %reduce-scatter.5.cloned.1.call-done = bf16[4,4,48,2,16]{2,4,3,1,0:T(8,128)(2,1)} async-done(((bf16[32,4,48,2,16]{2,4,3,1,0:T(8,128)(2,1)}), bf16[4,4,48,2,16]{2,4,3,1,0:T(8,128)(2,1)}) %reduce-scatter.5.cloned.1.call-update) | async-done | bytes 49168 | tf_op jit(solution)/shard_map/reduce_scatter | solution.py:107
  410.0 3.2 copy.153
  413.2 3.5 reshape.127
  416.8 200.1 %all-reduce.7.cloned.1.call-done = f32[2304,128]{1,0:T(8,128)} async-done(((f32[2304,128]{1,0:T(8,128)}), f32[2304,128]{1,0:T(8,128)}) %all-reduce.7.cloned.1.call-update) | async-done | bytes 1179664
  618.9 1.7 fusion.29
  (94 shorter events, 36.2 us)
Async XLA Ops:
  6.5 1.4 copy-start
  6.5 54.7 %reduce-scatter.3.cloned.1.call-start = ((), (), s32[]{:S(2)}) async-start(), calls=%async_computation.3 | async-start | bytes 1179648 | tf_op jit(solution)/shard_map/reduce_scatter | solution.py:107
  6.8 4.8 copy-start.4
  6.8 4.8 copy-start.6
  18.8 254.0 %all-reduce.5.cloned.1.call-start = ((), (), s32[]{:S(2)}) async-start(), calls=%async_computation.5 | async-start | bytes 2359296
  72.7 201.5 %copy-start.1 = (f32[36,2,16,16,4]{0,4,3,2,1:T(4,128)S(1)}, f32[36,2,16,16,4]{0,4,3,2,1:T(4,128)}, u32[]{:S(2)}) copy-start(f32[36,2,16,16,4]{0,4,3,2,1:T(4,128)} %param.7) | copy-start | bytes 884740
  334.5 9.2 %copy-start.10 = (bf16[16,16]{1,0:T(8,128)(2,1)S(1)}, bf16[16,16]{1,0:T(8,128)(2,1)}, u32[]{:S(2)}) copy-start(bf16[16,16]{1,0:T(8,128)(2,1)} %param.6) | copy-start | bytes 1540
  336.7 16.3 %all-to-all-start = ((bf16[8,2,6144]{2,1,0:T(2,128)(2,1)}), bf16[8,2,6144]{2,1,0:T(2,128)(2,1)S(1)}, u32[]{:S(2)}, u32[]{:S(2)}) async-start(bf16[8,2,6144]{2,1,0:T(2,128)(2,1)} %reshape.151), calls=%async_computation.1 | async-start | bytes 393216 | tf_op jit(solution)/shard_map/all_to_all | solution.py:165
  343.2 62.0 %reduce-scatter.5.cloned.1.call-start = ((), (), s32[]{:S(2)}) async-start(), calls=%async_computation.4 | async-start | bytes 1179648 | tf_op jit(solution)/shard_map/reduce_scatter | solution.py:107
  363.0 0.8 copy-start.5
  363.0 0.8 copy-start.7
  374.7 242.2 %all-reduce.7.cloned.1.call-start = ((), (), s32[]{:S(2)}) async-start(), calls=%async_computation.6 | async-start | bytes 2359296
  413.2 204.5 %copy-start.8 = (f32[36,16,4]{0,2,1:T(4,128)S(1)}, f32[36,16,4]{0,2,1:T(4,128)}, u32[]{:S(2)}) copy-start(f32[36,16,4]{0,2,1:T(4,128)} %get-tuple-element.25) | copy-start | bytes 27652
  413.2 204.5 %copy-start.9 = (f32[36,16,4]{0,2,1:T(4,128)S(1)}, f32[36,16,4]{0,2,1:T(4,128)}, u32[]{:S(2)}) copy-start(f32[36,16,4]{0,2,1:T(4,128)} %get-tuple-element.28) | copy-start | bytes 27652
  416.7 201.3 %copy-start.2 = (f32[36,2,16,16,4]{0,4,3,2,1:T(4,128)S(1)}, f32[36,2,16,16,4]{0,4,3,2,1:T(4,128)}, u32[]{:S(2)}) copy-start(f32[36,2,16,16,4]{0,4,3,2,1:T(4,128)} %param.7) | copy-start | bytes 884740
  617.7 1.2 copy-start.3
Sparse Core Ops, SparseCore 0:
  19.0 42.2 reduce-scatter.2
  72.9 199.8 all-reduce.4
  374.8 30.3 reduce-scatter.4
  416.9 199.9 all-reduce.6
where the time goes:
time: 634 us; the launch traced here: 627 us
  waiting for transfers between devices  477 us (75%)
  blocking collectives  51.3 us (8%)
  local copies, waits for them, and re-layouts  46.1 us (7%)
  matrix products  27 us (4%)
  between operations  14.5 us (2%)
  starting transfers between devices  7.18 us (1%)
    unnamed x6, waiting for transfers between devices  398 us
    reduce_scatter x2, waiting for transfers between devices, to_owners(): lax.psum_scatter(jnp.transpose(jnp.stack([real_out, imag_out], 2), (4, 0,...  72.4 us
    all_gather x1, blocking collectives, on_device(): gathered = lax.all_gather(flat_mixed, 'gx', axis=0, tiled=True)  51.3 us
    unnamed x35, local copies, waits for them, and re-layouts  13.7 us
  transfers between devices with their start and end apart: 5, of which 5 were waited for; matrix products, arithmetic and copies ran while one was open for 1% of the time, Pallas kernels for 0%

commit v1 on v0

v1 whole, which is shorter than its diff:
```python
import functools
import math

import jax
import jax.numpy as jnp
import ml_dtypes
import numpy as np
from jax import lax
from jax.experimental import pallas as pl
from jax.experimental.pallas import tpu as pltpu
from jax.sharding import PartitionSpec as P

C = 16
MX = 48
MY = 48
MZ = 32
NX = 256
NY = 192
NZ = 512
GX = 64
GY = 8
XL = NX // GX
YL = NY // GY
KZL = MZ // GY
ROWS = XL * YL
BF = jnp.bfloat16
F32 = jnp.float32
LANES = 128
CH2 = 24
CH6 = 40


def angle(a, b, n):
    return (2.0 * np.pi / n) * ((np.asarray(a)[:, None] * np.asarray(b)[None, :]) % n).astype(np.float64)


def split(table):
    table = np.asarray(table, np.float64)
    high = table.astype(ml_dtypes.bfloat16)
    low = (table - high.astype(np.float64)).astype(ml_dtypes.bfloat16)
    return high, low


def z_tables():
    a = angle(np.arange(NZ), np.arange(MZ), NZ).astype(np.float32)
    tab = np.stack([np.cos(a), -np.sin(a)], 0).astype(ml_dtypes.bfloat16)
    tab = tab.reshape(2, NZ, GY, KZL)
    fwd = np.zeros((2, NZ, 2, 2, GY, KZL), ml_dtypes.bfloat16)
    inv = np.zeros((2, 2, GY, KZL, 2, NZ), ml_dtypes.bfloat16)
    for h in range(2):
        fwd[h, :, :, h] = np.transpose(tab, (1, 0, 2, 3))
        inv[:, h, :, :, h, :] = np.transpose(tab, (0, 2, 3, 1))
    return fwd.reshape(2 * NZ, LANES), inv.reshape(LANES, 2 * NZ)


def y_forward_table():
    a = angle(np.arange(MY), np.arange(NY), NY)
    ch, cl = split(np.cos(a) / math.sqrt(NY))
    sh, sl = split(np.sin(a) / math.sqrt(NY))
    return np.concatenate([ch, cl, sh, sl], 0)


def x_forward_table():
    a = angle(np.arange(MX), np.arange(NX), NX)
    parts = []
    for t in split(np.cos(a) / math.sqrt(NX)) + split(np.sin(a) / math.sqrt(NX)):
        t = t.reshape(MX, GX, 1, XL)
        parts.append(np.concatenate([t, t], 2).reshape(MX, GX * 2 * XL))
    return np.concatenate(parts, 0)


def x_inverse_table():
    a = angle(np.arange(NX), np.arange(MX), NX)
    t = np.concatenate(split(np.cos(a)) + split(np.sin(a)), 1)
    out = np.zeros((GX, 8, 4 * MX), ml_dtypes.bfloat16)
    out[:, :XL] = t.reshape(GX, XL, 4 * MX)
    return out.reshape(GX * 8, 4 * MX)


def y_inverse_table():
    a = angle(np.arange(NY), np.arange(MY), NY)
    factor = 1.0 / math.sqrt(MX * MY * MZ)
    return np.concatenate(split(np.cos(a) * factor) + split(np.sin(a) * factor), 1)


def expand_table():
    e = np.zeros((2, C, KZL, 8, 2, 2, C, KZL), ml_dtypes.bfloat16)
    for r in range(2):
        for c in range(C):
            for k in range(KZL):
                e[r, c, k, c // 2, r, c % 2, :, k] = 1.0
    return e.reshape(LANES, 8 * 2 * LANES)


def dot(a, b):
    return jnp.dot(a, b, preferred_element_type=F32)


def dot_t(a, b, **kw):
    return lax.dot_general(a, b, (((1,), (1,)), ((), ())), preferred_element_type=F32, **kw)


def lane_of(shape):
    return lax.broadcasted_iota(jnp.int32, shape, len(shape) - 1)


def exchange_groups(arrays):
    arrays = list(arrays)
    lane = lane_of(arrays[0].shape)
    for bit in range(3):
        stride = 4 << bit
        clear = (lane & stride) == 0
        for i in range(8):
            if i & (1 << bit):
                continue
            lo, hi = arrays[i], arrays[i | (1 << bit)]
            arrays[i] = jnp.where(clear, lo, pltpu.roll(hi, stride, 1))
            arrays[i | (1 << bit)] = jnp.where(clear, pltpu.roll(lo, LANES - stride, 1), hi)
    return arrays


def times_minus_i(v):
    return pltpu.roll(v, 64, 1) * jnp.where(lane_of(v.shape) < 64, 1.0, -1.0)


def times_plus_i(v):
    return pltpu.roll(v, 64, 1) * jnp.where(lane_of(v.shape) < 64, -1.0, 1.0)


def write_z_modes(even, odd, w_ref, out_ref):
    modes = dot(even, w_ref[0:NZ, :]) + dot(odd, w_ref[NZ : 2 * NZ, :])
    modes = modes / math.sqrt(NZ)
    parts = exchange_groups([modes[16 * i : 16 * i + 16] for i in range(8)])
    for p in range(GY):
        out_ref[p] = parts[p].astype(BF)


def k1(field_ref, w_ref, out_ref):
    x = field_ref[...].reshape(C * 16, NZ)
    write_z_modes(x[0:128], x[128:256], w_ref, out_ref)


def y_transform(in_ref, ty_ref):
    full = in_ref[...].astype(F32)
    out = []
    for x in range(XL):
        rows = jnp.concatenate([full[p, YL * x : YL * x + YL, :] for p in range(GY)], 0).astype(BF)
        t = dot(ty_ref[...], rows)
        cos, sin = t[0:48] + t[48:96], t[96:144] + t[144:192]
        out.append(cos + times_minus_i(sin))
    return out


def k2(in_ref, spec_ref, ty_ref, out_ref, scratch):
    quarter = lax.axis_index("gx") % 4
    j = lax.broadcasted_iota(jnp.int32, (MY, 36), 0)
    t = lax.broadcasted_iota(jnp.int32, (MY, 36), 1) + 36 * quarter
    t = t - jnp.where(t >= 48, 48, 0) - jnp.where(t >= 96, 48, 0)
    select = (t == j).astype(BF)
    for k in range(16):
        block = spec_ref[128 * k : 128 * k + 128, :].astype(BF)
        scratch[pl.ds(k, MY, stride=CH2), :] = dot_t(select, block)
    for x, v in enumerate(y_transform(in_ref, ty_ref)):
        high = v.astype(BF).astype(F32)
        scratch[pl.ds(16 + x, MY, stride=CH2), :] = high
        scratch[pl.ds(20 + x, MY, stride=CH2), :] = v - high
    out_ref[0 : MY * CH2, :] = scratch[...].astype(BF)
    out_ref[MY * CH2 : GX * CH2, :] = jnp.zeros(((GX - MY) * CH2, LANES), BF)


def k3(in_ref, tx_ref, e_ref, tinv_ref, out_ref, scratch):
    ky = lax.axis_index("gx")
    data = in_ref[:, 16:24, :].astype(F32).reshape(GX * 8, LANES).astype(BF)
    t = dot(tx_ref[...], data)
    fwd = t[0:48] + t[48:96] + times_minus_i(t[96:144] + t[144:192])
    high = fwd.astype(BF)
    low = (fwd - high.astype(F32)).astype(BF)
    both = jnp.concatenate([high, low], 0)
    source = (
        jnp.where(ky >= 36, 1, 0),
        1 + jnp.where(ky >= 24, 1, 0),
        2 + jnp.where(ky >= 12, 1, 0),
    )
    for kx in range(MX):
        block = in_ref[4 * (kx // 3) + source[kx % 3], 0:16, :]
        scratch[16 * kx : 16 * kx + 16, :] = block.astype(F32)
    mixed_r = jnp.zeros((MX, LANES), F32)
    mixed_i = jnp.zeros((MX, LANES), F32)
    for k in range(8):
        wide = dot(both, e_ref[:, 256 * k : 256 * k + 256])
        wide = wide[0:48] + wide[48:96]
        fr, fi = wide[:, 0:128], wide[:, 128:256]
        wr = scratch[pl.ds(k, MX, stride=16), :]
        wi = scratch[pl.ds(8 + k, MX, stride=16), :]
        mixed_r += wr * fr - wi * fi
        mixed_i += wr * fi + wi * fr
    mixed_r += pltpu.roll(mixed_r, 64, 1)
    mixed_i += pltpu.roll(mixed_i, 64, 1)
    mixed = jnp.where(lane_of(mixed_r.shape) < 64, mixed_r, mixed_i)
    mixed = mixed.astype(BF)
    turned = times_plus_i(mixed.astype(F32)).astype(BF)
    row = lax.broadcasted_iota(jnp.int32, (GX * 8, 2 * MX), 0)
    col = lax.broadcasted_iota(jnp.int32, (GX * 8, 2 * MX), 1)
    owner = row // 8
    part = row % 8
    quarter = owner % 4
    back_one = jnp.where(quarter == 1, jnp.where(ky >= 36, 1, 0), 0)
    back_one += jnp.where(quarter == 2, jnp.where(ky >= 24, 1, 0), 0)
    kx_of = 3 * (owner // 4) + jnp.minimum(quarter, 2) - back_one
    wanted = jnp.where(part == 4, kx_of, jnp.where(part == 5, kx_of + MX, -1))
    select = (col == wanted).astype(BF)
    result = dot(tinv_ref[...], jnp.concatenate([mixed, mixed, turned, turned], 0))
    result += dot(select, both)
    out_ref[...] = result.astype(BF)


def k4(in_ref, ty_ref, out_ref, scratch):
    scratch[...] = in_ref[0 : 8 * MY, :].astype(F32)
    for x in range(XL):
        v = scratch[pl.ds(x, MY, stride=8), :]
        b = v.astype(BF)
        s = times_plus_i(v).astype(BF)
        w = dot(ty_ref[...], jnp.concatenate([b, b, s, s], 0))
        for p in range(GY):
            out_ref[p, YL * x : YL * x + YL, :] = w[YL * p : YL * p + YL].astype(BF)


def slope(pre):
    inner = 0.7978845608 * (pre + 0.044715 * pre * pre * pre)
    t = jnp.tanh(inner)
    return 0.5 * (1.0 + t) + 0.5 * pre * (1.0 - t * t) * 0.7978845608 * (1.0 + 3.0 * 0.044715 * pre * pre)


def k5(waves_ref, field_ref, cot_ref, pw_ref, w_ref, zt_ref, out_ref, kron):
    @pl.when(pl.program_id(0) == 0)
    def _():
        group = lax.broadcasted_iota(jnp.int32, (256, C), 0) // 16
        member = lax.broadcasted_iota(jnp.int32, (256, C), 1)
        one_hot = (group == member).astype(BF)
        wide = dot_t(one_hot, pw_ref[...]).astype(BF)
        wide = dot_t(wide, one_hot)
        r = lax.broadcasted_iota(jnp.int32, (256, 256), 0) % 16
        s = lax.broadcasted_iota(jnp.int32, (256, 256), 1) % 16
        kron[...] = jnp.where(r == s, wide, 0.0).astype(BF)

    groups = exchange_groups([waves_ref[p].astype(F32) for p in range(GY)])
    waves = jnp.concatenate(groups, 0).astype(BF)
    x = field_ref[...].reshape(C * 16, NZ)
    halves = []
    for h in range(2):
        pre = dot(waves, zt_ref[:, NZ * h : NZ * h + NZ])
        pre += dot(kron[128 * h : 128 * h + 128, :], x)
        cot = cot_ref[8 * h : 8 * h + 8].reshape(128, NZ).astype(F32)
        halves.append((cot * slope(pre)).astype(BF))
    write_z_modes(halves[0], halves[1], w_ref, out_ref)


def k6(in_ref, ty_ref, cs_ref, out_ref):
    base = XL * lax.axis_index("gx")
    values = y_transform(in_ref, ty_ref)
    turned = [times_minus_i(v) for v in values]

    def body(g, carry):
        rows = []
        for r in range(3):
            kx = 3 * g + r
            acc = None
            for x in range(XL):
                at = (kx * (base + x)) & (NX - 1)
                term = values[x] * cs_ref[at] + turned[x] * cs_ref[NX + at]
                acc = term if acc is None else acc + term
            rows.append(acc)
        a, b, c = rows
        out_ref[4 * g] = a[0:40].astype(BF)
        out_ref[4 * g + 1] = jnp.concatenate([b[0:24], a[32:48]], 0).astype(BF)
        out_ref[4 * g + 2] = jnp.concatenate([b[24:48], c[0:16]], 0).astype(BF)
        out_ref[4 * g + 3] = c[8:48].astype(BF)
        return carry

    lax.fori_loop(0, MX // 3, body, 0)


def k7(in_ref, fwd_ref, spec_ref, mom_ref, out_ref):
    quarter = lax.axis_index("gx") % 4
    total = in_ref[0].astype(F32)
    for g in range(1, GX):
        total += in_ref[g].astype(F32)
    to = lax.broadcasted_iota(jnp.int32, (LANES, CH6), 0)
    at = lax.broadcasted_iota(jnp.int32, (LANES, CH6), 1)
    source = jnp.where(
        quarter == 1,
        jnp.where(to < 12, to + 28, to - 12),
        jnp.where(quarter == 3, to + 4, to),
    )
    source = jnp.where(to < 36, source, -1)
    select = (at == source).astype(F32)
    grads = jnp.dot(select, total, precision=lax.Precision.HIGHEST, preferred_element_type=F32)
    to = lax.broadcasted_iota(jnp.int32, (LANES, 8 * MY), 0)
    at = lax.broadcasted_iota(jnp.int32, (LANES, 8 * MY), 1)
    t = to + 36 * quarter
    t = t - jnp.where(t >= 48, 48, 0) - jnp.where(t >= 96, 48, 0)
    hit = ((at // 8) == t) & ((at % 8) >= 4) & ((at % 8) < 6) & (to < 36)
    fwd = dot(hit.astype(BF), fwd_ref[0 : 8 * MY, :])
    grads = grads.T[:, 0:36]
    fwd = fwd.T[:, 0:36]
    grad_r, grad_i = grads[0:64], grads[64:128]
    for c in range(C):
        fr = fwd[4 * c : 4 * c + 4]
        fi = fwd[64 + 4 * c : 68 + 4 * c]
        fr = jnp.concatenate([fr] * 16, 0)
        fi = jnp.concatenate([fi] * 16, 0)
        d_real = grad_r * fr + grad_i * fi
        d_imag = grad_i * fr - grad_r * fi
        out_ref[0, c] = mom_ref[0, c] - 0.25 * (d_real + 2.0 * C * spec_ref[0, c])
        out_ref[1, c] = mom_ref[1, c] - 0.25 * (d_imag + 2.0 * C * spec_ref[1, c])


def call(body, out, *args, scratch=(), smem=()):
    specs = [
        pl.BlockSpec(memory_space=pltpu.SMEM if i in smem else pltpu.VMEM) for i in range(len(args))
    ]
    return pl.pallas_call(
        body,
        out_shape=out,
        in_specs=specs,
        out_specs=pl.BlockSpec(memory_space=pltpu.VMEM),
        scratch_shapes=list(scratch),
        compiler_params=pltpu.CompilerParams(vmem_limit_bytes=40 * 1024 * 1024),
    )(*args)


def whole(shape):
    return pl.BlockSpec(shape, lambda i: (0,) * len(shape))


def swap(value, axis):
    return lax.all_to_all(value, axis, split_axis=0, concat_axis=0, tiled=True)


def on_device(field, pointwise, spectral, momentum, cotangent):
    field = field.reshape(C, ROWS, NZ)
    cotangent = cotangent.reshape(C, ROWS, NZ)
    spectral = jnp.transpose(spectral, (1, 2, 3, 4, 0))
    momentum = jnp.transpose(momentum, (1, 2, 3, 4, 0))
    zf, zi = z_tables()
    zf, zi = jnp.asarray(zf), jnp.asarray(zi)
    ty = jnp.asarray(y_forward_table())
    steps = ROWS // 16
    zshape = jax.ShapeDtypeStruct((GY, ROWS, LANES), BF)
    zblock = pl.BlockSpec((GY, 16, LANES), lambda i: (0, i, 0))
    fblock = pl.BlockSpec((C, 16, NZ), lambda i: (0, i, 0))
    zmodes = pl.pallas_call(
        k1,
        out_shape=zshape,
        grid=(steps,),
        in_specs=[fblock, whole((2 * NZ, LANES))],
        out_specs=zblock,
    )(field, zf)
    zmodes = swap(zmodes, "gy")
    sent = call(
        k2,
        jax.ShapeDtypeStruct((GX * CH2, LANES), BF),
        zmodes,
        spectral.reshape(2 * C * C * KZL, 36),
        ty,
        scratch=[pltpu.VMEM((MY * CH2, LANES), F32)],
    )
    got = swap(sent.reshape(GX, CH2, LANES), "gx")
    sent = call(
        k3,
        jax.ShapeDtypeStruct((GX * 8, LANES), BF),
        got,
        jnp.asarray(x_forward_table()),
        jnp.asarray(expand_table()),
        jnp.asarray(x_inverse_table()),
        scratch=[pltpu.VMEM((MX * 16, LANES), F32)],
    )
    back = swap(sent.reshape(GX, 8, LANES), "gx").reshape(GX * 8, LANES)
    waves = call(
        k4,
        zshape,
        back,
        jnp.asarray(y_inverse_table()),
        scratch=[pltpu.VMEM((8 * MY, LANES), F32)],
    )
    waves = swap(waves, "gy")
    zgrads = pl.pallas_call(
        k5,
        out_shape=zshape,
        grid=(steps,),
        in_specs=[
            zblock,
            fblock,
            fblock,
            whole((C, C)),
            whole((2 * NZ, LANES)),
            whole((LANES, 2 * NZ)),
        ],
        out_specs=zblock,
        scratch_shapes=[pltpu.VMEM((256, 256), BF)],
    )(waves, field, cotangent, pointwise, zf, zi)
    zgrads = swap(zgrads, "gy")
    turn = 2.0 * np.pi / NX * np.arange(NX)
    cs = np.concatenate([np.cos(turn), np.sin(turn)]) / math.sqrt(NX)
    partial = call(
        k6,
        jax.ShapeDtypeStruct((GX, CH6, LANES), BF),
        zgrads,
        ty,
        jnp.asarray(cs.astype(np.float32)),
        smem=(2,),
    )
    partial = swap(partial, "gx")
    result = call(
        k7,
        jax.ShapeDtypeStruct((2, C, C * KZL, 36), F32),
        partial,
        back,
        spectral.reshape(2, C, C * KZL, 36),
        momentum.reshape(2, C, C * KZL, 36),
    )
    result = result.reshape(2, C, C, KZL, 36)
    return jnp.transpose(result, (4, 0, 1, 2, 3))


def solution(mesh):
    in_specs = (
        P(None, "gx", "gy", None),
        P(),
        P("gx", None, None, None, "gy"),
        P("gx", None, None, None, "gy"),
        P(None, "gx", "gy", None),
    )
    out_specs = P("gx", None, None, None, "gy")
    return jax.shard_map(
        on_device, mesh=mesh, in_specs=in_specs, out_specs=out_specs, check_vma=False
    )
```

time: 634 us -> 136 us (0.21)
  waiting for transfers between devices: 477 us -> 0 us
  blocking collectives: 51.3 us -> 116 us
  local copies, waits for them, and re-layouts: 46.1 us -> 0.03 us
  matrix products: 27 us -> 0 us
  Pallas kernels: 0 us -> 19.9 us
  between operations: 14.5 us -> 0.05 us
  starting transfers between devices: 7.18 us -> 0 us
    unnamed x6 -> x0, waiting for transfers between devices: 398 us -> none
    all_to_all x0 -> x6, blocking collectives: none -> 116 us  [swap(): return lax.all_to_all(value, axis, split_axis=0, concat_axis=0, tiled=True)]
    reduce_scatter x2 -> x0, waiting for transfers between devices: 72.4 us -> none  [to_owners(): lax.psum_scatter(jnp.transpose(jnp.stack([real_out, imag_out], 2), (4, 0,...]
    all_gather x1 -> x0, blocking collectives: 51.3 us -> none  [on_device(): gathered = lax.all_gather(flat_mixed, 'gx', axis=0, tiled=True)]
    dot_general x28 -> x0, matrix products: 27 us -> none  [the longest x1 5.51 us: on_device(): jnp.einsum('xyrck,rkz->cxyz', waves, ztable, preferred_element_type=jnp.f...]
    pallas_call x0 -> x7, Pallas kernels: none -> 19.9 us  [the longest x1 8.67 us: on_device(): pl.pallas_call(k5, out_shape=zshape, grid=(steps,), in_specs=[zblock, fbl...]
    unnamed x35 -> x16, local copies, waits for them, and re-layouts: 13.7 us -> 0.03 us
    reshape x4 -> x0, local copies, waits for them, and re-layouts: 10.4 us -> none  [the longest x2 7.01 us: x_modes(): flat = forward_x(ycoef, kxs, xpos, total_x).reshape(MX * MY, 2 * width)]
  transfers between devices with their start and end apart: 5 -> 0, of which waited for: 5 -> 0; matrix products, arithmetic and copies ran while one was open for 1% -> 0% of each run, Pallas kernels for 0% -> 0%
where the time goes in v1:
time: 136 us
  blocking collectives  116 us (85%)
  Pallas kernels  19.9 us (15%)
    all_to_all x6, blocking collectives, swap(): return lax.all_to_all(value, axis, split_axis=0, concat_axis=0, tiled=True)  116 us
    pallas_call x1, Pallas kernels, on_device(): pl.pallas_call(k5, out_shape=zshape, grid=(steps,), in_specs=[zblock, fbl...  8.67 us
    pallas_call x1, Pallas kernels, on_device(): pl.pallas_call(k1, out_shape=zshape, grid=(steps,), in_specs=[fblock, who...  5.64 us
    pallas_call x5, Pallas kernels, call(): pl.pallas_call(body, out_shape=out, in_specs=specs, out_specs=pl.BlockSpe...  5.54 us

profile of v1, /device:TPU:1, one launch (start us, length us, event | category | flops | bytes accessed | tf_op | source)
XLA Modules:
  0.0 135.6 jit_solution(5086383439639942377)
XLA Ops:
  0.0 0.0 copy-start.3
  0.0 0.0 copy-start
  0.0 5.6 %shard_map.127 = bf16[8,96,128]{2,1,0:T(8,128)(2,1)} custom-call(bf16[16,96,512]{2,1,0:T(8,128)(2,1)} %bitcast.23, bf16[1024,128]{1,0:T(8,128)(2,1)} %constant.16.clone.w_ref), custom_call_target="tpu_custom_call" | custom-call | tf_op jit(solution)/shard_map/pallas_call | solution.py:352
  5.7 16.5 %all_to_all.30.in_ref = bf16[8,96,128]{2,1,0:T(8,128)(2,1)S(1)} all-to-all(bf16[8,96,128]{2,1,0:T(8,128)(2,1)} %shard_map.127), channel_id=1, replica_groups=mesh['gx'=64,'gy'=8] {'gy'}, dimensions={0} | all-to-all | bytes 393216 | tf_op jit(solution)/shard_map/all_to_all | solution.py:337
  22.2 0.0 copy-done.3
  22.2 0.0 copy-done
  22.2 0.7 shard_map.128
  22.9 0.0 copy-start.6
  22.9 31.0 %all_to_all.31.in_ref = bf16[64,24,128]{2,1,0:T(8,128)(2,1)S(1)} all-to-all(bf16[64,24,128]{2,1,0:T(8,128)(2,1)S(1)} %bitcast.18), channel_id=1, replica_groups=mesh['gx'=64,'gy'=8] {'gx'}, dimensions={0} | all-to-all | bytes 786432 | tf_op jit(solution)/shard_map/all_to_all | solution.py:337
  53.9 0.0 copy-done.2
  53.9 0.0 copy-done.4
  53.9 0.0 copy-done.5
  53.9 1.0 shard_map.129
  54.9 16.5 %all_to_all.32 = bf16[64,8,128]{2,1,0:T(8,128)(2,1)S(1)} all-to-all(bf16[64,8,128]{2,1,0:T(8,128)(2,1)S(1)} %bitcast.22), channel_id=1, replica_groups=mesh['gx'=64,'gy'=8] {'gx'}, dimensions={0} | all-to-all | bytes 262144 | tf_op jit(solution)/shard_map/all_to_all | solution.py:337
  71.4 0.0 copy-done.6
  71.4 0.3 shard_map.130
  71.8 13.0 %all_to_all.33.waves_ref = bf16[8,96,128]{2,1,0:T(8,128)(2,1)} all-to-all(bf16[8,96,128]{2,1,0:T(8,128)(2,1)S(1)} %shard_map.130), channel_id=1, replica_groups=mesh['gx'=64,'gy'=8] {'gy'}, dimensions={0} | all-to-all | bytes 393216 | tf_op jit(solution)/shard_map/all_to_all | solution.py:337
  84.8 8.7 %shard_map.131 = bf16[8,96,128]{2,1,0:T(8,128)(2,1)} custom-call(bf16[8,96,128]{2,1,0:T(8,128)(2,1)} %all_to_all.33.waves_ref, bf16[16,96,512]{2,1,0:T(8,128)(2,1)} %bitcast.24, bf16[16,96,512]{2,1,0:T(8,128)(2,1)} %bitcast.25, bf16[16,16]{1,0:T(8,128)(2,1)} %pw_ref.1, bf16[1024,128]{1,0:T(8,128)(2,1)} %constant.16.clone.w_ref, ...), custom_call_target="tpu_custom_call" | custom-call | tf_op jit(solution)/shard_map/pallas_call | solution.py:387
  93.5 11.8 %all_to_all.34.in_ref = bf16[8,96,128]{2,1,0:T(8,128)(2,1)S(1)} all-to-all(bf16[8,96,128]{2,1,0:T(8,128)(2,1)} %shard_map.131), channel_id=1, replica_groups=mesh['gx'=64,'gy'=8] {'gy'}, dimensions={0} | all-to-all | bytes 393216 | tf_op jit(solution)/shard_map/all_to_all | solution.py:337
  105.3 0.0 copy-done.7
  105.3 1.8 %shard_map.132 = bf16[64,40,128]{2,1,0:T(8,128)(2,1)S(1)} custom-call(bf16[8,96,128]{2,1,0:T(8,128)(2,1)S(1)} %all_to_all.34.in_ref, bf16[192,192]{1,0:T(8,128)(2,1)S(1)} %copy-done.3, f32[512]{0:T(512)S(1)} %copy-done.7), custom_call_target="tpu_custom_call" | custom-call | tf_op jit(solution)/shard_map/pallas_call | solution.py:322
  107.0 26.8 %all_to_all.35.in_ref = bf16[64,40,128]{2,1,0:T(8,128)(2,1)S(1)} all-to-all(bf16[64,40,128]{2,1,0:T(8,128)(2,1)S(1)} %shard_map.132), channel_id=1, replica_groups=mesh['gx'=64,'gy'=8] {'gx'}, dimensions={0} | all-to-all | bytes 1310720 | tf_op jit(solution)/shard_map/all_to_all | solution.py:337
  133.8 0.0 copy-done.1
  133.8 1.8 %shard_map.133 = f32[2,16,64,36]{3,2,1,0:T(8,128)} custom-call(bf16[64,40,128]{2,1,0:T(8,128)(2,1)S(1)} %all_to_all.35.in_ref, bf16[512,128]{1,0:T(8,128)(2,1)S(1)} %bitcast.20, f32[2,16,64,36]{3,2,1,0:T(8,128)S(1)} %bitcast.17, f32[2,16,64,36]{3,2,1,0:T(8,128)S(1)} %bitcast.21), custom_call_target="tpu_custom_call" | custom-call | tf_op jit(solution)/shard_map/pallas_call | solution.py:322
  (5 shorter events, 0.0 us)
Async XLA Ops:
  0.0 22.2 %copy-start.3 = (bf16[192,192]{1,0:T(8,128)(2,1)S(1)}, bf16[192,192]{1,0:T(8,128)(2,1)}, u32[]{:S(2)}) copy-start(bf16[192,192]{1,0:T(8,128)(2,1)} %constant.18.clone.ty_ref) | copy-start | bytes 221188
  0.0 22.2 %copy-start = (f32[36,2,16,16,4]{0,4,3,2,1:T(4,128)S(1)}, f32[36,2,16,16,4]{0,4,3,2,1:T(4,128)}, u32[]{:S(2)}) copy-start(f32[36,2,16,16,4]{0,4,3,2,1:T(4,128)} %param.15) | copy-start | bytes 884740
  5.6 48.3 %copy-start.2 = (bf16[128,2048]{1,0:T(8,128)(2,1)S(1)}, bf16[128,2048]{1,0:T(8,128)(2,1)}, u32[]{:S(2)}) copy-start(bf16[128,2048]{1,0:T(8,128)(2,1)} %constant.20.clone.e_ref) | copy-start | bytes 1572868
  5.7 48.3 %copy-start.4 = (bf16[512,192]{1,0:T(8,128)(2,1)S(1)}, bf16[512,192]{1,0:T(8,128)(2,1)}, u32[]{:S(2)}) copy-start(bf16[512,192]{1,0:T(8,128)(2,1)} %constant.21.clone.tinv_ref) | copy-start | bytes 589828
  5.7 48.3 %copy-start.5 = (bf16[192,512]{1,0:T(8,128)(2,1)S(1)}, bf16[192,512]{1,0:T(8,128)(2,1)}, u32[]{:S(2)}) copy-start(bf16[192,512]{1,0:T(8,128)(2,1)} %constant.19.clone.tx_ref) | copy-start | bytes 589828
  22.9 48.5 %copy-start.6 = (bf16[192,192]{1,0:T(8,128)(2,1)S(1)}, bf16[192,192]{1,0:T(8,128)(2,1)}, u32[]{:S(2)}) copy-start(bf16[192,192]{1,0:T(8,128)(2,1)} %constant.22.clone.ty_ref) | copy-start | bytes 221188
  84.8 20.5 %copy-start.7 = (f32[512]{0:T(512)S(1)}, f32[512]{0:T(512)}, u32[]{:S(2)}) copy-start(f32[512]{0:T(512)} %constant.23.clone.cs_ref) | copy-start | bytes 6148
  93.5 40.4 %copy-start.1 = (f32[36,2,16,16,4]{0,4,3,2,1:T(4,128)S(1)}, f32[36,2,16,16,4]{0,4,3,2,1:T(4,128)}, u32[]{:S(2)}) copy-start(f32[36,2,16,16,4]{0,4,3,2,1:T(4,128)} %param.16) | copy-start | bytes 884740

commit v2 on v1

v2 whole, which is shorter than its diff:
```python
import math

import jax
import jax.numpy as jnp
import ml_dtypes
import numpy as np
from jax import lax
from jax.experimental import pallas as pl
from jax.experimental.pallas import tpu as pltpu
from jax.sharding import PartitionSpec as P

C = 16
MX = 48
MY = 48
MZ = 32
NX = 256
NY = 192
NZ = 512
GX = 64
GY = 8
XL = NX // GX
YL = NY // GY
KZL = MZ // GY
ROWS = XL * YL
BF = jnp.bfloat16
F32 = jnp.float32
LANES = 128
OWNED = MX * MY // GX
TRIPLES = np.arange(48).reshape(16, 3).T.reshape(48)


def angle(a, b, n):
    return (2.0 * np.pi / n) * ((np.asarray(a)[:, None] * np.asarray(b)[None, :]) % n).astype(np.float64)


def split(table):
    table = np.asarray(table, np.float64)
    high = table.astype(ml_dtypes.bfloat16)
    low = (table - high.astype(np.float64)).astype(ml_dtypes.bfloat16)
    return high, low


def z_tables():
    a = angle(np.arange(NZ), np.arange(MZ), NZ).astype(np.float32)
    tab = np.stack([np.cos(a), -np.sin(a)], 0).astype(ml_dtypes.bfloat16)
    tab = tab.reshape(2, NZ, GY, KZL)
    mid = np.zeros((2, NZ, KZL, 2, 2, GY), ml_dtypes.bfloat16)
    own = np.zeros((2, NZ, 2, 2, GY, KZL), ml_dtypes.bfloat16)
    inv = np.zeros((KZL, 2, 2, GY, 2, NZ), ml_dtypes.bfloat16)
    for h in range(2):
        mid[h, :, :, :, h] = np.transpose(tab, (1, 3, 0, 2))
        own[h, :, :, h] = np.transpose(tab, (1, 0, 2, 3))
        inv[:, :, h, :, h, :] = np.transpose(tab, (3, 0, 2, 1))
    return mid.reshape(2 * NZ, LANES), own.reshape(2 * NZ, LANES), inv.reshape(LANES, 2 * NZ)


def y_forward_table(kys):
    a = angle(kys, np.arange(NY), NY)
    return np.concatenate(split(np.cos(a) / math.sqrt(NY)) + split(np.sin(a) / math.sqrt(NY)), 0)


def x_forward_table():
    xs = np.arange(NX).reshape(GX, XL).T.reshape(NX)
    a = angle(TRIPLES, xs, NX)
    return np.concatenate(split(np.cos(a) / math.sqrt(NX)) + split(np.sin(a) / math.sqrt(NX)), 0)


def x_inverse_table():
    a = angle(np.arange(NX), TRIPLES, NX)
    return np.concatenate(split(np.cos(a)) + split(np.sin(a)), 1)


def y_inverse_table():
    a = angle(np.arange(NY), TRIPLES, NY)
    factor = 1.0 / math.sqrt(MX * MY * MZ)
    return np.concatenate(split(np.cos(a) * factor) + split(np.sin(a) * factor), 1)


def expand_table():
    e = np.zeros((4, 2, 2, 8, 3, 2, 2, 8, C), ml_dtypes.bfloat16)
    for i in range(3):
        for r in range(2):
            for h in range(2):
                for c in range(8):
                    e[i, r, h, c, i, h, r, c, :] = 1.0
    return e.reshape(LANES, 6 * 2 * LANES)


def reorder_table():
    t = np.zeros((KZL, 2, C, 2, C, KZL), ml_dtypes.bfloat16)
    for k in range(KZL):
        for r in range(2):
            for c in range(C):
                t[k, r, c, r, c, k] = 1.0
    return t.reshape(LANES, LANES)


def dot(a, b):
    return jnp.dot(a, b, preferred_element_type=F32)


def dot_t(a, b):
    return lax.dot_general(a, b, (((1,), (1,)), ((), ())), preferred_element_type=F32)


def lane_of(shape):
    return lax.broadcasted_iota(jnp.int32, shape, len(shape) - 1)


def exchange(arrays, first):
    arrays = list(arrays)
    lane = lane_of(arrays[0].shape)
    bit = 1
    while bit < len(arrays):
        stride = first * bit
        clear = (lane & stride) == 0
        for i in range(len(arrays)):
            if i & bit:
                continue
            lo, hi = arrays[i], arrays[i | bit]
            arrays[i] = jnp.where(clear, lo, pltpu.roll(hi, stride, 1))
            arrays[i | bit] = jnp.where(clear, pltpu.roll(lo, LANES - stride, 1), hi)
        bit *= 2
    return arrays


def partner(v, stride):
    real = (lane_of(v.shape) & stride) == 0
    if stride == 64:
        return pltpu.roll(v, 64, 1), real
    return jnp.where(real, pltpu.roll(v, LANES - stride, 1), pltpu.roll(v, stride, 1)), real


def times_minus_i(v, stride):
    other, real = partner(v, stride)
    return jnp.where(real, other, -other)


def times_plus_i(v, stride):
    other, real = partner(v, stride)
    return jnp.where(real, -other, other)


def z_modes(even, odd, w_ref, first):
    modes = dot(even, w_ref[0:NZ, :]) + dot(odd, w_ref[NZ : 2 * NZ, :])
    modes = modes * (1.0 / math.sqrt(NZ))
    n = modes.shape[0] // 8
    return exchange([modes[n * i : n * i + n] for i in range(8)], first)


def k1(field_ref, w_ref, out_ref):
    even = field_ref[0:8].reshape(8 * ROWS, NZ)
    odd = field_ref[8:16].reshape(8 * ROWS, NZ)
    for p, v in enumerate(z_modes(even, odd, w_ref, 1)):
        out_ref[p] = v.astype(BF)


def y_transform(in_ref, ty_ref, stride):
    full = in_ref[...].astype(F32)
    out = []
    for x in range(XL):
        rows = jnp.concatenate([full[p, YL * x : YL * x + YL, :] for p in range(GY)], 0).astype(BF)
        t = dot(ty_ref[...], rows)
        cos, sin = t[0:48] + t[48:96], t[96:144] + t[144:192]
        out.append(cos + times_minus_i(sin, stride))
    return out


def ky_of(value, quarter):
    t = value + OWNED * quarter
    return t - jnp.where(t >= 48, 48, 0) - jnp.where(t >= 96, 48, 0)


def k2(in_ref, spec_ref, ty_ref, out_ref, scratch):
    quarter = lax.axis_index("gx") % 4
    row = lax.broadcasted_iota(jnp.int32, (MY, OWNED), 0)
    mode = ky_of(lax.broadcasted_iota(jnp.int32, (MY, OWNED), 1), quarter)
    select = (mode == 3 * (row % 16) + row // 16).astype(BF)
    for k in range(4):
        for b in range(KZL):
            block = spec_ref[pl.ds(512 * k + b, LANES, stride=KZL), :].astype(BF)
            moved = dot_t(select, block)
            for i in range(3):
                scratch[pl.ds(16 * b + 4 + 4 * i + k, 16, stride=64), :] = moved[16 * i : 16 * i + 16]
    for x, v in enumerate(y_transform(in_ref, ty_ref, 16)):
        parts = [v[0:16], v[16:32], v[32:48], jnp.zeros((16, LANES), F32)]
        for b, part in enumerate(exchange(parts, 32)):
            scratch[pl.ds(16 * b + x, 16, stride=64), :] = part
    out_ref[...] = scratch[...].astype(BF)


def k3(in_ref, tx_ref, e_ref, tinv_ref, out_ref, scratch):
    a = lax.axis_index("gx") // 4
    scratch[...] = in_ref[...].astype(F32)
    data = jnp.concatenate([scratch[pl.ds(x, GX, stride=16), :] for x in range(XL)], 0).astype(BF)
    t = dot(tx_ref[...], data)
    fwd = t[0:48] + t[48:96] + times_minus_i(t[96:144] + t[144:192], 16)
    high = fwd.astype(BF)
    low = (fwd - high.astype(F32)).astype(BF)
    both = jnp.concatenate([high, low], 0)
    source = (
        jnp.where(a >= 12, 1, 0),
        1 + jnp.where(a >= 8, 1, 0),
        2 + jnp.where(a >= 4, 1, 0),
    )

    def weights(i, k):
        at = 4 + 4 * i + k
        return jnp.concatenate(
            [scratch[pl.ds(16 * source[r] + at, 16, stride=64), :] for r in range(3)], 0
        )

    group = lane_of((MX, LANES)) // 16
    mixed = jnp.zeros((MX, LANES), F32)
    for i in range(3):
        sums = [0.0, 0.0]
        for h in range(2):
            at = 256 * (2 * i + h)
            wide = dot(both, e_ref[:, at : at + 256])
            wide = wide[0:48] + wide[48:96]
            fr, fi = wide[:, 0:128], wide[:, 128:256]
            wr, wi = weights(i, h), weights(i, 2 + h)
            sums[0] += wr * fr - wi * fi
            sums[1] += wr * fi + wi * fr
        for r in range(2):
            v = sums[r]
            for stride in (64, 32, 16):
                v = v + pltpu.roll(v, stride, 1)
            mixed = jnp.where(group == 2 * i + r, v, mixed)
    mixed = mixed.astype(BF)
    turned = times_plus_i(mixed.astype(F32), 16).astype(BF)
    moved = [
        jnp.where(group >= 6, pltpu.roll(high.astype(F32), 96 - 32 * i, 1), 0.0)
        for i in range(3)
    ]
    moved = jnp.concatenate(moved, 0).astype(BF)
    row = lax.broadcasted_iota(jnp.int32, (NX, 3 * MX), 0)
    col = lax.broadcasted_iota(jnp.int32, (NX, 3 * MX), 1)
    owner = row // 4
    quarter = owner % 4
    back_one = jnp.where(quarter == 1, jnp.where(a >= 12, 1, 0), 0)
    back_one += jnp.where(quarter == 2, jnp.where(a >= 8, 1, 0), 0)
    r = jnp.minimum(quarter, 2) - back_one
    wanted = MX * (row % 4) + 16 * r + owner // 4
    select = (col == wanted).astype(BF)
    result = dot(tinv_ref[...], jnp.concatenate([mixed, mixed, turned, turned], 0))
    result += dot(select, moved)
    out_ref[...] = result.astype(BF)


def k4(in_ref, ty_ref, out_ref, fwd_ref, scratch):
    scratch[...] = in_ref[...].astype(F32)
    for x in range(XL):
        parts = [scratch[pl.ds(4 * b + x, 16, stride=16), :] for b in range(KZL)]
        parts = exchange(parts, 32)
        if x < 3:
            fwd_ref[16 * x : 16 * x + 16, :] = parts[3]
        v = jnp.concatenate(parts[0:3], 0)
        b = v.astype(BF)
        s = times_plus_i(v, 16).astype(BF)
        w = dot(ty_ref[...], jnp.concatenate([b, b, s, s], 0))
        for p in range(GY):
            out_ref[p, YL * x : YL * x + YL, :] = w[YL * p : YL * p + YL].astype(BF)


def slope(pre):
    square = pre * pre
    t = jnp.tanh(pre * (0.7978845608 + 0.7978845608 * 0.044715 * square))
    ramp = pre * (0.5 * 0.7978845608 + 1.5 * 0.7978845608 * 0.044715 * square)
    return (0.5 + 0.5 * t) + (1.0 - t * t) * ramp


def k5(waves_ref, field_ref, cot_ref, pw_ref, w_ref, zt_ref, out_ref, kron, grad):
    group = lax.broadcasted_iota(jnp.int32, (256, C), 0) // 16
    member = lax.broadcasted_iota(jnp.int32, (256, C), 1)
    one_hot = (group == member).astype(BF)
    wide = dot_t(dot_t(one_hot, pw_ref[...]).astype(BF), one_hot)
    r = lax.broadcasted_iota(jnp.int32, (256, 256), 0) % 16
    s = lax.broadcasted_iota(jnp.int32, (256, 256), 1) % 16
    kron[...] = jnp.where(r == s, wide, 0.0).astype(BF)
    for n in range(ROWS // 16):
        rows = slice(16 * n, 16 * n + 16)
        parts = exchange([waves_ref[p, rows, :].astype(F32) for p in range(GY)], 1)
        waves = jnp.concatenate(parts, 0).astype(BF)
        x = field_ref[:, rows, :].reshape(C * 16, NZ)
        for h in range(2):
            pre = dot(waves, zt_ref[:, NZ * h : NZ * h + NZ])
            pre += dot(kron[128 * h : 128 * h + 128, :], x)
            cot = cot_ref[8 * h : 8 * h + 8, rows, :].reshape(128, NZ).astype(F32)
            grad[8 * h : 8 * h + 8, rows, :] = (cot * slope(pre)).astype(BF).reshape(8, 16, NZ)
    even = grad[0:8].reshape(8 * ROWS, NZ)
    odd = grad[8:16].reshape(8 * ROWS, NZ)
    for p, v in enumerate(z_modes(even, odd, w_ref, 4)):
        out_ref[p] = v.astype(BF)


def k6(in_ref, ty_ref, cs_ref, out_ref):
    base = XL * lax.axis_index("gx")
    values = y_transform(in_ref, ty_ref, 64)
    turned = [times_minus_i(v, 64) for v in values]

    def body(g, carry):
        for r in range(3):
            kx = 3 * g + r
            acc = None
            for x in range(XL):
                at = (kx * (base + x)) & (NX - 1)
                term = values[x] * cs_ref[at] + turned[x] * cs_ref[NX + at]
                acc = term if acc is None else acc + term
            out_ref[pl.ds(pl.multiple_of(48 * kx, 16), 48), :] = acc.astype(BF)
        return carry

    lax.fori_loop(0, MX // 3, body, 0)


def k7(in_ref, fwd_ref, reorder_ref, spec_ref, mom_ref, out_ref, scratch):
    quarter = lax.axis_index("gx") % 4
    pair = 2 * OWNED
    total = in_ref[0:pair, :].astype(F32)
    for g in range(1, GX // 2):
        total += in_ref[pair * g : pair * g + pair, :].astype(F32)
    scratch[0:pair, :] = total
    scratch[pair : pair + 8, :] = jnp.zeros((8, LANES), F32)
    grads = scratch[0:40, :] + scratch[OWNED : OWNED + 40, :]
    grads = jnp.concatenate([grads, jnp.zeros((LANES - 40, LANES), F32)], 0)
    row = lax.broadcasted_iota(jnp.int32, (LANES, MY), 0)
    col = lax.broadcasted_iota(jnp.int32, (LANES, MY), 1)
    hit = (ky_of(row, quarter) == 3 * (col % 16) + col // 16) & (row < OWNED)
    fwd = dot(hit.astype(BF), fwd_ref[...].astype(BF)).astype(BF)
    fwd = dot(fwd, reorder_ref[...])
    grads = grads.T[:, 0:OWNED]
    fwd = fwd.T[:, 0:OWNED]
    grad_r, grad_i = grads[0:64], grads[64:128]
    for c in range(C):
        fr = fwd[4 * c : 4 * c + 4]
        fi = fwd[64 + 4 * c : 68 + 4 * c]
        fr = jnp.concatenate([fr] * 16, 0)
        fi = jnp.concatenate([fi] * 16, 0)
        d_real = grad_r * fr + grad_i * fi
        d_imag = grad_i * fr - grad_r * fi
        out_ref[0, c] = mom_ref[0, c] - 0.25 * (d_real + 2.0 * C * spec_ref[0, c])
        out_ref[1, c] = mom_ref[1, c] - 0.25 * (d_imag + 2.0 * C * spec_ref[1, c])


def call(body, out, *args, scratch=(), smem=()):
    specs = [
        pl.BlockSpec(memory_space=pltpu.SMEM if i in smem else pltpu.VMEM) for i in range(len(args))
    ]
    vmem = pl.BlockSpec(memory_space=pltpu.VMEM)
    return pl.pallas_call(
        body,
        out_shape=out,
        in_specs=specs,
        out_specs=jax.tree.map(lambda _: vmem, out),
        scratch_shapes=list(scratch),
        compiler_params=pltpu.CompilerParams(vmem_limit_bytes=40 * 1024 * 1024),
    )(*args)


def swap(value, axis):
    return lax.all_to_all(value, axis, split_axis=0, concat_axis=0, tiled=True)


def on_device(field, pointwise, spectral, momentum, cotangent):
    field = field.reshape(C, ROWS, NZ)
    cotangent = cotangent.reshape(C, ROWS, NZ)
    spectral = jnp.transpose(spectral, (1, 2, 3, 4, 0))
    momentum = jnp.transpose(momentum, (1, 2, 3, 4, 0))
    z_mid, z_own, z_inv = [jnp.asarray(t) for t in z_tables()]
    zshape = jax.ShapeDtypeStruct((GY, ROWS, LANES), BF)

    zmodes = swap(call(k1, zshape, field, z_mid), "gy")
    sent = call(
        k2,
        jax.ShapeDtypeStruct((GX * 16, LANES), BF),
        zmodes,
        spectral.reshape(2 * C * C * KZL, OWNED),
        jnp.asarray(y_forward_table(TRIPLES)),
        scratch=[pltpu.VMEM((GX * 16, LANES), F32)],
    )
    got = swap(sent.reshape(GX, 16, LANES), "gx").reshape(GX * 16, LANES)
    sent = call(
        k3,
        jax.ShapeDtypeStruct((NX, LANES), BF),
        got,
        jnp.asarray(x_forward_table()),
        jnp.asarray(expand_table()),
        jnp.asarray(x_inverse_table()),
        scratch=[pltpu.VMEM((GX * 16, LANES), F32)],
    )
    back = swap(sent.reshape(GX, XL, LANES), "gx").reshape(NX, LANES)
    waves, fwd = call(
        k4,
        (zshape, jax.ShapeDtypeStruct((MY, LANES), F32)),
        back,
        jnp.asarray(y_inverse_table()),
        scratch=[pltpu.VMEM((NX, LANES), F32)],
    )
    zgrads = call(
        k5,
        zshape,
        swap(waves, "gy"),
        field,
        cotangent,
        pointwise,
        z_own,
        z_inv,
        scratch=[pltpu.VMEM((256, 256), BF), pltpu.VMEM((C, ROWS, NZ), BF)],
    )
    turn = 2.0 * np.pi / NX * np.arange(NX)
    cs = np.concatenate([np.cos(turn), np.sin(turn)]) / math.sqrt(NX)
    partial = call(
        k6,
        jax.ShapeDtypeStruct((MX * MY, LANES), BF),
        swap(zgrads, "gy"),
        jnp.asarray(y_forward_table(np.arange(MY))),
        jnp.asarray(cs.astype(np.float32)),
        smem=(2,),
    )
    partial = swap(partial.reshape(GX, OWNED // 4, 4, LANES), "gx").reshape(MX * MY, LANES)
    result = call(
        k7,
        jax.ShapeDtypeStruct((2, C, C * KZL, OWNED), F32),
        partial,
        fwd,
        jnp.asarray(reorder_table()),
        spectral.reshape(2, C, C * KZL, OWNED),
        momentum.reshape(2, C, C * KZL, OWNED),
        scratch=[pltpu.VMEM((2 * OWNED + 8, LANES), F32)],
    )
    result = result.reshape(2, C, C, KZL, OWNED)
    return jnp.transpose(result, (4, 0, 1, 2, 3))


def solution(mesh):
    in_specs = (
        P(None, "gx", "gy", None),
        P(),
        P("gx", None, None, None, "gy"),
        P("gx", None, None, None, "gy"),
        P(None, "gx", "gy", None),
    )
    out_specs = P("gx", None, None, None, "gy")
    return jax.shard_map(
        on_device, mesh=mesh, in_specs=in_specs, out_specs=out_specs, check_vma=False
    )
```

time: 136 us -> 121 us (0.89)
  Pallas kernels: 19.9 us -> 9.55 us
  blocking collectives: 116 us -> 109 us
  local copies, waits for them, and re-layouts: 0.03 us -> 2.44 us
    pallas_call x7, Pallas kernels: 19.9 us -> 9.55 us  [call(): pl.pallas_call(body, out_shape=out, in_specs=specs, out_specs=jax.tree.ma...]
    all_to_all x6, blocking collectives: 116 us -> 109 us  [swap(): return lax.all_to_all(value, axis, split_axis=0, concat_axis=0, tiled=True)]
    unnamed x16 -> x34, local copies, waits for them, and re-layouts: 0.03 us -> 2.44 us
where the time goes in v2:
time: 121 us
  blocking collectives  109 us (90%)
  Pallas kernels  9.55 us (8%)
  local copies, waits for them, and re-layouts  2.44 us (2%)
    all_to_all x6, blocking collectives, swap(): return lax.all_to_all(value, axis, split_axis=0, concat_axis=0, tiled=True)  109 us
    pallas_call x7, Pallas kernels, call(): pl.pallas_call(body, out_shape=out, in_specs=specs, out_specs=jax.tree.ma...  9.55 us
    unnamed x34, local copies, waits for them, and re-layouts  2.44 us

profile of v2, /device:TPU:1, one launch (start us, length us, event | category | flops | bytes accessed | tf_op | source)
XLA Modules:
  0.0 121.0 jit_solution(7127810380837537856)
XLA Ops:
  0.0 1.4 %copy-done = bf16[16,4,24,512]{3,2,1,0:T(8,128)(2,1)S(1)} copy-done((bf16[16,4,24,512]{3,2,1,0:T(8,128)(2,1)S(1)}, bf16[16,4,24,512]{3,2,1,0:T(8,128)(2,1)}, u32[]{:S(2)}) %copy-start) | copy-done | bytes 1572888
  1.4 0.9 copy-done.8
  2.4 0.8 shard_map.154
  3.2 0.0 copy-start.5
  3.2 0.0 copy-start.11
  3.2 16.3 %all_to_all.30.in_ref = bf16[8,96,128]{2,1,0:T(8,128)(2,1)S(1)} all-to-all(bf16[8,96,128]{2,1,0:T(8,128)(2,1)S(1)} %shard_map.154), channel_id=1, replica_groups=mesh['gx'=64,'gy'=8] {'gy'}, dimensions={0} | all-to-all | bytes 393216 | tf_op jit(solution)/shard_map/all_to_all | solution.py:361
  19.5 0.0 copy-start.6
  19.5 0.0 copy-start.7
  19.5 0.0 copy-start.15
  19.6 1.0 shard_map.155
  20.5 29.1 %all_to_all.31 = bf16[64,16,128]{2,1,0:T(8,128)(2,1)S(1)} all-to-all(bf16[64,16,128]{2,1,0:T(8,128)(2,1)S(1)} %bitcast.26), channel_id=1, replica_groups=mesh['gx'=64,'gy'=8] {'gx'}, dimensions={0} | all-to-all | bytes 524288 | tf_op jit(solution)/shard_map/all_to_all | solution.py:361
  49.6 1.1 shard_map.156
  50.7 14.6 %all_to_all.32 = bf16[64,4,128]{2,1,0:T(4,128)(2,1)S(1)} all-to-all(bf16[64,4,128]{2,1,0:T(4,128)(2,1)S(1)} %bitcast.30), channel_id=1, replica_groups=mesh['gx'=64,'gy'=8] {'gx'}, dimensions={0} | all-to-all | bytes 131072 | tf_op jit(solution)/shard_map/all_to_all | solution.py:361
  65.3 0.5 shard_map.157
  65.9 12.4 %all_to_all.33.waves_ref = bf16[8,96,128]{2,1,0:T(8,128)(2,1)S(1)} all-to-all(bf16[8,96,128]{2,1,0:T(8,128)(2,1)S(1)} %get-tuple-element.7), channel_id=1, replica_groups=mesh['gx'=64,'gy'=8] {'gy'}, dimensions={0} | all-to-all | bytes 393216 | tf_op jit(solution)/shard_map/all_to_all | solution.py:361
  78.3 0.0 copy-start.10
  78.3 0.0 copy-start.16
  78.3 2.8 %shard_map.158 = bf16[8,96,128]{2,1,0:T(8,128)(2,1)S(1)} custom-call(bf16[8,96,128]{2,1,0:T(8,128)(2,1)S(1)} %all_to_all.33.waves_ref, bf16[16,96,512]{2,1,0:T(8,128)(2,1)S(1)} %bitcast.20, bf16[16,96,512]{2,1,0:T(8,128)(2,1)S(1)} %bitcast.25, bf16[16,16]{1,0:T(8,128)(2,1)S(1)} %copy-done.15, bf16[1024,128]{1,0:T(8,128)(2,1)S(1)} %copy-done.7, ...), custom_call_target="tpu_custom_call" | custom-call | tf_op jit(solution)/shard_map/pallas_call | solution.py:350
  81.1 0.0 copy-start.4
  81.2 0.0 copy-start.14
  81.2 10.9 %all_to_all.34.in_ref = bf16[8,96,128]{2,1,0:T(8,128)(2,1)S(1)} all-to-all(bf16[8,96,128]{2,1,0:T(8,128)(2,1)S(1)} %shard_map.158), channel_id=1, replica_groups=mesh['gx'=64,'gy'=8] {'gy'}, dimensions={0} | all-to-all | bytes 393216 | tf_op jit(solution)/shard_map/all_to_all | solution.py:361
  92.1 1.7 %shard_map.159 = bf16[2304,128]{1,0:T(8,128)(2,1)S(1)} custom-call(bf16[8,96,128]{2,1,0:T(8,128)(2,1)S(1)} %all_to_all.34.in_ref, bf16[192,192]{1,0:T(8,128)(2,1)S(1)} %copy-done.10, f32[512]{0:T(512)S(1)} %copy-done.16), custom_call_target="tpu_custom_call" | custom-call | tf_op jit(solution)/shard_map/pallas_call | solution.py:350
  93.8 25.5 %all_to_all.35 = bf16[64,9,4,128]{3,2,1,0:T(4,128)(2,1)S(1)} all-to-all(bf16[64,9,4,128]{3,2,1,0:T(4,128)(2,1)S(1)} %bitcast.23), channel_id=1, replica_groups=mesh['gx'=64,'gy'=8] {'gx'}, dimensions={0} | all-to-all | bytes 1179648 | tf_op jit(solution)/shard_map/all_to_all | solution.py:361
  119.3 1.6 %shard_map.160 = f32[2,16,64,36]{3,2,1,0:T(8,128)} custom-call(bf16[2304,128]{1,0:T(8,128)(2,1)S(1)} %bitcast.24, f32[48,128]{1,0:T(8,128)S(1)} %get-tuple-element.8.fwd_ref, bf16[128,128]{1,0:T(8,128)(2,1)S(1)} %copy-done.14, f32[2,16,64,36]{3,2,1,0:T(8,128)S(1)} %bitcast.22, f32[2,16,64,36]{3,2,1,0:T(8,128)S(1)} %bitcast.28), custom_call_target="tpu_custom_call" | custom-call | tf_op jit(solution)/shard_map/pallas_call | solution.py:350
  (23 shorter events, 0.0 us)
Async XLA Ops:
  0.0 1.4 %copy-start = (bf16[16,4,24,512]{3,2,1,0:T(8,128)(2,1)S(1)}, bf16[16,4,24,512]{3,2,1,0:T(8,128)(2,1)}, u32[]{:S(2)}) copy-start(bf16[16,4,24,512]{3,2,1,0:T(8,128)(2,1)} %param.16) | copy-start | bytes 4718596
  1.4 0.9 copy-start.8
  2.4 17.1 %copy-start.2 = (f32[36,2,16,16,4]{0,4,3,2,1:T(4,128)S(1)}, f32[36,2,16,16,4]{0,4,3,2,1:T(4,128)}, u32[]{:S(2)}) copy-start(f32[36,2,16,16,4]{0,4,3,2,1:T(4,128)} %param.18) | copy-start | bytes 884740
  2.4 17.1 %copy-start.12 = (bf16[192,192]{1,0:T(8,128)(2,1)S(1)}, bf16[192,192]{1,0:T(8,128)(2,1)}, u32[]{:S(2)}) copy-start(bf16[192,192]{1,0:T(8,128)(2,1)} %constant.25.clone.ty_ref) | copy-start | bytes 221188
  2.4 47.3 %copy-start.9 = (bf16[256,192]{1,0:T(8,128)(2,1)S(1)}, bf16[256,192]{1,0:T(8,128)(2,1)}, u32[]{:S(2)}) copy-start(bf16[256,192]{1,0:T(8,128)(2,1)} %constant.28.clone.tinv_ref) | copy-start | bytes 294916
  2.4 63.0 %copy-start.13 = (bf16[192,192]{1,0:T(8,128)(2,1)S(1)}, bf16[192,192]{1,0:T(8,128)(2,1)}, u32[]{:S(2)}) copy-start(bf16[192,192]{1,0:T(8,128)(2,1)} %constant.29.clone.ty_ref) | copy-start | bytes 221188
  3.2 46.5 %copy-start.5 = (bf16[128,1536]{1,0:T(8,128)(2,1)S(1)}, bf16[128,1536]{1,0:T(8,128)(2,1)}, u32[]{:S(2)}) copy-start(bf16[128,1536]{1,0:T(8,128)(2,1)} %constant.27.clone.e_ref) | copy-start | bytes 1179652
  3.2 46.5 %copy-start.11 = (bf16[192,256]{1,0:T(8,128)(2,1)S(1)}, bf16[192,256]{1,0:T(8,128)(2,1)}, u32[]{:S(2)}) copy-start(bf16[192,256]{1,0:T(8,128)(2,1)} %constant.26.clone.tx_ref) | copy-start | bytes 294916
  19.5 58.7 %copy-start.1 = (bf16[16,4,24,512]{3,2,1,0:T(8,128)(2,1)S(1)}, bf16[16,4,24,512]{3,2,1,0:T(8,128)(2,1)}, u32[]{:S(2)}) copy-start(bf16[16,4,24,512]{3,2,1,0:T(8,128)(2,1)} %param.16) | copy-start | bytes 4718596
  19.5 58.7 %copy-start.3 = (bf16[16,4,24,512]{3,2,1,0:T(8,128)(2,1)S(1)}, bf16[16,4,24,512]{3,2,1,0:T(8,128)(2,1)}, u32[]{:S(2)}) copy-start(bf16[16,4,24,512]{3,2,1,0:T(8,128)(2,1)} %param.20) | copy-start | bytes 4718596
  19.5 58.7 %copy-start.6 = (bf16[128,1024]{1,0:T(8,128)(2,1)S(1)}, bf16[128,1024]{1,0:T(8,128)(2,1)}, u32[]{:S(2)}) copy-start(bf16[128,1024]{1,0:T(8,128)(2,1)} %constant.24.clone.zt_ref) | copy-start | bytes 786436
  19.5 58.7 %copy-start.7 = (bf16[1024,128]{1,0:T(8,128)(2,1)S(1)}, bf16[1024,128]{1,0:T(8,128)(2,1)}, u32[]{:S(2)}) copy-start(bf16[1024,128]{1,0:T(8,128)(2,1)} %constant.23.clone.w_ref) | copy-start | bytes 786436
  19.5 58.7 %copy-start.15 = (bf16[16,16]{1,0:T(8,128)(2,1)S(1)}, bf16[16,16]{1,0:T(8,128)(2,1)}, u32[]{:S(2)}) copy-start(bf16[16,16]{1,0:T(8,128)(2,1)} %pw_ref.1) | copy-start | bytes 1540
  78.3 13.8 %copy-start.10 = (bf16[192,192]{1,0:T(8,128)(2,1)S(1)}, bf16[192,192]{1,0:T(8,128)(2,1)}, u32[]{:S(2)}) copy-start(bf16[192,192]{1,0:T(8,128)(2,1)} %constant.30.clone.ty_ref) | copy-start | bytes 221188
  78.3 13.8 %copy-start.16 = (f32[512]{0:T(512)S(1)}, f32[512]{0:T(512)}, u32[]{:S(2)}) copy-start(f32[512]{0:T(512)} %constant.31.clone.cs_ref) | copy-start | bytes 6148
  81.1 38.2 %copy-start.4 = (f32[36,2,16,16,4]{0,4,3,2,1:T(4,128)S(1)}, f32[36,2,16,16,4]{0,4,3,2,1:T(4,128)}, u32[]{:S(2)}) copy-start(f32[36,2,16,16,4]{0,4,3,2,1:T(4,128)} %param.19) | copy-start | bytes 884740
  81.2 38.2 %copy-start.14 = (bf16[128,128]{1,0:T(8,128)(2,1)S(1)}, bf16[128,128]{1,0:T(8,128)(2,1)}, u32[]{:S(2)}) copy-start(bf16[128,128]{1,0:T(8,128)(2,1)} %constant.32.clone.reorder_ref) | copy-start | bytes 98308

commit v3 on v2

--- a/solution.py
+++ b/solution.py
@@ -26,7 +26,9 @@
 F32 = jnp.float32
 LANES = 128
 OWNED = MX * MY // GX
+GXS = ("chip", "core")
 TRIPLES = np.arange(48).reshape(16, 3).T.reshape(48)
+PAIRS = np.arange(48).reshape(24, 2).T.reshape(48)
 
 
 def angle(a, b, n):
@@ -45,13 +47,13 @@
     tab = np.stack([np.cos(a), -np.sin(a)], 0).astype(ml_dtypes.bfloat16)
     tab = tab.reshape(2, NZ, GY, KZL)
     mid = np.zeros((2, NZ, KZL, 2, 2, GY), ml_dtypes.bfloat16)
-    own = np.zeros((2, NZ, 2, 2, GY, KZL), ml_dtypes.bfloat16)
+    half = np.zeros((2, NZ, 2, 2, GY, KZL), ml_dtypes.bfloat16)
     inv = np.zeros((KZL, 2, 2, GY, 2, NZ), ml_dtypes.bfloat16)
     for h in range(2):
         mid[h, :, :, :, h] = np.transpose(tab, (1, 3, 0, 2))
-        own[h, :, :, h] = np.transpose(tab, (1, 0, 2, 3))
+        half[h, :, h] = np.transpose(tab, (1, 0, 2, 3))
         inv[:, :, h, :, h, :] = np.transpose(tab, (3, 0, 2, 1))
-    return mid.reshape(2 * NZ, LANES), own.reshape(2 * NZ, LANES), inv.reshape(LANES, 2 * NZ)
+    return mid.reshape(2 * NZ, LANES), half.reshape(2 * NZ, LANES), inv.reshape(LANES, 2 * NZ)
 
 
 def y_forward_table(kys):
@@ -74,6 +76,18 @@
     a = angle(np.arange(NY), TRIPLES, NY)
     factor = 1.0 / math.sqrt(MX * MY * MZ)
     return np.concatenate(split(np.cos(a) * factor) + split(np.sin(a) * factor), 1)
+
+
+def partial_tables():
+    shift = (4 * np.arange(2)[:, None] + np.arange(2)[None, :]).reshape(4)
+    lanes = 2 * (np.arange(LANES) // 64)
+    a = (2.0 * np.pi / NX) * np.arange(MX)[:, None, None] * (shift[:, None] + lanes[None, :])[None]
+    cos, sin = np.cos(a) / math.sqrt(NX), np.sin(a) / math.sqrt(NX)
+    near = np.concatenate([cos, sin], 1).reshape(8 * MX, LANES)
+    turn = np.concatenate([-sin, cos], 1).reshape(8 * MX, LANES)
+    whole = 2.0 * np.pi / NX * np.arange(NX)
+    whole = np.concatenate([np.cos(whole), np.sin(whole)])
+    return [t.astype(np.float32) for t in (near, turn, whole)]
 
 
 def expand_table():
@@ -141,24 +155,36 @@
     return jnp.where(real, -other, other)
 
 
-def z_modes(even, odd, w_ref, first):
+def z_modes(even, odd, w_ref):
     modes = dot(even, w_ref[0:NZ, :]) + dot(odd, w_ref[NZ : 2 * NZ, :])
     modes = modes * (1.0 / math.sqrt(NZ))
-    n = modes.shape[0] // 8
-    return exchange([modes[n * i : n * i + n] for i in range(8)], first)
-
-
-def k1(field_ref, w_ref, out_ref):
-    even = field_ref[0:8].reshape(8 * ROWS, NZ)
-    odd = field_ref[8:16].reshape(8 * ROWS, NZ)
-    for p, v in enumerate(z_modes(even, odd, w_ref, 1)):
+    return [modes[i : i + ROWS] for i in range(0, modes.shape[0], ROWS)]
+
+
+def k1(field_ref, w_ref, out_ref, x_ref, t_ref, sems):
+    table = pltpu.make_async_copy(w_ref, t_ref, sems.at[8])
+    table.start()
+    copies = []
+    for n in range(4):
+        for h in range(2):
+            part = pl.ds(8 * h + 2 * n, 2)
+            copies.append(pltpu.make_async_copy(field_ref.at[part], x_ref.at[part], sems.at[2 * n + h]))
+            copies[-1].start()
+    table.wait()
+    modes = []
+    for n in range(4):
+        copies[2 * n].wait()
+        copies[2 * n + 1].wait()
+        even = x_ref[2 * n : 2 * n + 2].reshape(2 * ROWS, NZ)
+        odd = x_ref[8 + 2 * n : 10 + 2 * n].reshape(2 * ROWS, NZ)
+        modes += z_modes(even, odd, t_ref)
+    for p, v in enumerate(exchange(modes, 1)):
         out_ref[p] = v.astype(BF)
 
 
-def y_transform(in_ref, ty_ref, stride):
-    full = in_ref[...].astype(F32)
+def y_transform(full, ty_ref, stride):
     out = []
-    for x in range(XL):
+    for x in range(full.shape[1] // YL):
         rows = jnp.concatenate([full[p, YL * x : YL * x + YL, :] for p in range(GY)], 0).astype(BF)
         t = dot(ty_ref[...], rows)
         cos, sin = t[0:48] + t[48:96], t[96:144] + t[144:192]
@@ -171,8 +197,12 @@
     return t - jnp.where(t >= 48, 48, 0) - jnp.where(t >= 96, 48, 0)
 
 
+def place():
+    return 2 * lax.axis_index("chip") + lax.axis_index("core")
+
+
 def k2(in_ref, spec_ref, ty_ref, out_ref, scratch):
-    quarter = lax.axis_index("gx") % 4
+    quarter = place() % 4
     row = lax.broadcasted_iota(jnp.int32, (MY, OWNED), 0)
     mode = ky_of(lax.broadcasted_iota(jnp.int32, (MY, OWNED), 1), quarter)
     select = (mode == 3 * (row % 16) + row // 16).astype(BF)
@@ -182,7 +212,7 @@
             moved = dot_t(select, block)
             for i in range(3):
                 scratch[pl.ds(16 * b + 4 + 4 * i + k, 16, stride=64), :] = moved[16 * i : 16 * i + 16]
-    for x, v in enumerate(y_transform(in_ref, ty_ref, 16)):
+    for x, v in enumerate(y_transform(in_ref[...].astype(F32), ty_ref, 16)):
         parts = [v[0:16], v[16:32], v[32:48], jnp.zeros((16, LANES), F32)]
         for b, part in enumerate(exchange(parts, 32)):
             scratch[pl.ds(16 * b + x, 16, stride=64), :] = part
@@ -190,7 +220,7 @@
 
 
 def k3(in_ref, tx_ref, e_ref, tinv_ref, out_ref, scratch):
-    a = lax.axis_index("gx") // 4
+    a = place() // 4
     scratch[...] = in_ref[...].astype(F32)
     data = jnp.concatenate([scratch[pl.ds(x, GX, stride=16), :] for x in range(XL)], 0).astype(BF)
     t = dot(tx_ref[...], data)
@@ -290,39 +320,55 @@
             grad[8 * h : 8 * h + 8, rows, :] = (cot * slope(pre)).astype(BF).reshape(8, 16, NZ)
     even = grad[0:8].reshape(8 * ROWS, NZ)
     odd = grad[8:16].reshape(8 * ROWS, NZ)
-    for p, v in enumerate(z_modes(even, odd, w_ref, 4)):
-        out_ref[p] = v.astype(BF)
-
-
-def k6(in_ref, ty_ref, cs_ref, out_ref):
-    base = XL * lax.axis_index("gx")
-    values = y_transform(in_ref, ty_ref, 64)
-    turned = [times_minus_i(v, 64) for v in values]
-
-    def body(g, carry):
-        for r in range(3):
-            kx = 3 * g + r
-            acc = None
-            for x in range(XL):
-                at = (kx * (base + x)) & (NX - 1)
-                term = values[x] * cs_ref[at] + turned[x] * cs_ref[NX + at]
-                acc = term if acc is None else acc + term
-            out_ref[pl.ds(pl.multiple_of(48 * kx, 16), 48), :] = acc.astype(BF)
-        return carry
-
-    lax.fori_loop(0, MX // 3, body, 0)
+    for p, v in enumerate(exchange(z_modes(even, odd, w_ref), 4)):
+        for core, part in enumerate(exchange([v[0:48], v[48:96]], 64)):
+            out_ref[8 * core + p] = part.astype(BF)
+
+
+def k6(in_ref, ty_ref, near_ref, turn_ref, cs_ref, out_ref, factors):
+    chip = lax.axis_index("chip")
+    for kx in range(MX):
+        at = (8 * kx * chip) & (NX - 1)
+        rows = slice(8 * kx, 8 * kx + 8)
+        factors[rows, :] = near_ref[rows, :] * cs_ref[at] + turn_ref[rows, :] * cs_ref[NX + at]
+    full = in_ref[...].astype(F32)
+    values = []
+    for core in range(2):
+        values += y_transform(full[8 * core : 8 * core + 8], ty_ref, 32)
+    turned = [times_minus_i(v, 32) for v in values]
+    low = lane_of((24, LANES)) < 64
+
+    terms = values + turned
+    for kx in range(0, MX, 2):
+        rows = []
+        for at in (8 * kx, 8 * kx + 8):
+            acc = terms[0] * factors[at : at + 1, :]
+            for n in range(1, 8):
+                acc += terms[n] * factors[at + n : at + n + 1, :]
+            even, odd = acc[0:24], acc[24:48]
+            rows.append(jnp.where(low, even, odd) + pltpu.roll(jnp.where(low, odd, even), 64, 1))
+        out_ref[24 * kx : 24 * kx + 48, :] = jnp.concatenate(rows, 0).astype(BF)
 
 
 def k7(in_ref, fwd_ref, reorder_ref, spec_ref, mom_ref, out_ref, scratch):
-    quarter = lax.axis_index("gx") % 4
-    pair = 2 * OWNED
-    total = in_ref[0:pair, :].astype(F32)
-    for g in range(1, GX // 2):
-        total += in_ref[pair * g : pair * g + pair, :].astype(F32)
-    scratch[0:pair, :] = total
-    scratch[pair : pair + 8, :] = jnp.zeros((8, LANES), F32)
-    grads = scratch[0:40, :] + scratch[OWNED : OWNED + 40, :]
-    grads = jnp.concatenate([grads, jnp.zeros((LANES - 40, LANES), F32)], 0)
+    quarter = place() % 4
+    total = in_ref[0:72, :].astype(F32)
+    for g in range(1, 16):
+        total += in_ref[72 * g : 72 * g + 72, :].astype(F32)
+    scratch[0:72, :] = total
+    scratch[72:80, :] = jnp.zeros((8, LANES), F32)
+    total = scratch[0:40, :] + scratch[36:76, :]
+    row = lax.broadcasted_iota(jnp.int32, (2 * LANES, 40), 0)
+    col = lax.broadcasted_iota(jnp.int32, (2 * LANES, 40), 1)
+    mode = row % LANES
+    select = ((col == 18 * (row // LANES) + mode // 2) & (mode < OWNED)).astype(F32)
+    moved = jnp.dot(select, total, precision=lax.Precision.HIGHEST, preferred_element_type=F32)
+    first, second = moved[0:LANES], moved[LANES : 2 * LANES]
+    odd = lax.broadcasted_iota(jnp.int32, (LANES, LANES), 0) % 2
+    upper = lane_of((LANES, LANES)) // 64
+    grads = jnp.where(upper == 0, first, second)
+    other = jnp.where(upper == 0, pltpu.roll(first, 64, 1), pltpu.roll(second, 64, 1))
+    grads = jnp.where(upper == odd, grads, other)
     row = lax.broadcasted_iota(jnp.int32, (LANES, MY), 0)
     col = lax.broadcasted_iota(jnp.int32, (LANES, MY), 1)
     hit = (ky_of(row, quarter) == 3 * (col % 16) + col // 16) & (row < OWNED)
@@ -330,7 +376,8 @@
     fwd = dot(fwd, reorder_ref[...])
     grads = grads.T[:, 0:OWNED]
     fwd = fwd.T[:, 0:OWNED]
-    grad_r, grad_i = grads[0:64], grads[64:128]
+    grad_r = jnp.concatenate([grads[0:32], grads[64:96]], 0)
+    grad_i = jnp.concatenate([grads[32:64], grads[96:128]], 0)
     for c in range(C):
         fr = fwd[4 * c : 4 * c + 4]
         fi = fwd[64 + 4 * c : 68 + 4 * c]
@@ -342,9 +389,10 @@
         out_ref[1, c] = mom_ref[1, c] - 0.25 * (d_imag + 2.0 * C * spec_ref[1, c])
 
 
-def call(body, out, *args, scratch=(), smem=()):
+def call(body, out, *args, scratch=(), smem=(), hbm=()):
     specs = [
-        pl.BlockSpec(memory_space=pltpu.SMEM if i in smem else pltpu.VMEM) for i in range(len(args))
+        pl.BlockSpec(memory_space=pltpu.SMEM if i in smem else pltpu.HBM if i in hbm else pltpu.VMEM)
+        for i in range(len(args))
     ]
     vmem = pl.BlockSpec(memory_space=pltpu.VMEM)
     return pl.pallas_call(
@@ -366,10 +414,22 @@
     cotangent = cotangent.reshape(C, ROWS, NZ)
     spectral = jnp.transpose(spectral, (1, 2, 3, 4, 0))
     momentum = jnp.transpose(momentum, (1, 2, 3, 4, 0))
-    z_mid, z_own, z_inv = [jnp.asarray(t) for t in z_tables()]
+    z_mid, z_half, z_inv = [jnp.asarray(t) for t in z_tables()]
     zshape = jax.ShapeDtypeStruct((GY, ROWS, LANES), BF)
 
-    zmodes = swap(call(k1, zshape, field, z_mid), "gy")
+    zmodes = call(
+        k1,
+        zshape,
+        pltpu.with_memory_space_constraint(field, pltpu.HBM),
+        pltpu.with_memory_space_constraint(z_mid, pltpu.HBM),
+        hbm=(0, 1),
+        scratch=[
+            pltpu.VMEM((C, ROWS, NZ), BF),
+            pltpu.VMEM((2 * NZ, LANES), BF),
+            pltpu.SemaphoreType.DMA((9,)),
+        ],
+    )
+    zmodes = swap(zmodes, "gy")
     sent = call(
         k2,
         jax.ShapeDtypeStruct((GX * 16, LANES), BF),
@@ -378,7 +438,7 @@
         jnp.asarray(y_forward_table(TRIPLES)),
         scratch=[pltpu.VMEM((GX * 16, LANES), F32)],
     )
-    got = swap(sent.reshape(GX, 16, LANES), "gx").reshape(GX * 16, LANES)
+    got = swap(sent.reshape(GX, 16, LANES), GXS).reshape(GX * 16, LANES)
     sent = call(
         k3,
         jax.ShapeDtypeStruct((NX, LANES), BF),
@@ -388,7 +448,7 @@
         jnp.asarray(x_inverse_table()),
         scratch=[pltpu.VMEM((GX * 16, LANES), F32)],
     )
-    back = swap(sent.reshape(GX, XL, LANES), "gx").reshape(NX, LANES)
+    back = swap(sent.reshape(GX, XL, LANES), GXS).reshape(NX, LANES)
     waves, fwd = call(
         k4,
         (zshape, jax.ShapeDtypeStruct((MY, LANES), F32)),
@@ -398,26 +458,25 @@
     )
     zgrads = call(
         k5,
-        zshape,
+        jax.ShapeDtypeStruct((2 * GY, ROWS // 2, LANES), BF),
         swap(waves, "gy"),
         field,
         cotangent,
         pointwise,
-        z_own,
+        z_half,
         z_inv,
         scratch=[pltpu.VMEM((256, 256), BF), pltpu.VMEM((C, ROWS, NZ), BF)],
     )
-    turn = 2.0 * np.pi / NX * np.arange(NX)
-    cs = np.concatenate([np.cos(turn), np.sin(turn)]) / math.sqrt(NX)
     partial = call(
         k6,
-        jax.ShapeDtypeStruct((MX * MY, LANES), BF),
-        swap(zgrads, "gy"),
-        jnp.asarray(y_forward_table(np.arange(MY))),
-        jnp.asarray(cs.astype(np.float32)),
-        smem=(2,),
-    )
-    partial = swap(partial.reshape(GX, OWNED // 4, 4, LANES), "gx").reshape(MX * MY, LANES)
+        jax.ShapeDtypeStruct((MX * MY // 2, LANES), BF),
+        swap(zgrads, ("core", "gy")),
+        jnp.asarray(y_forward_table(PAIRS)),
+        *[jnp.asarray(t) for t in partial_tables()],
+        smem=(4,),
+        scratch=[pltpu.VMEM((8 * MX, LANES), F32)],
+    )
+    partial = swap(partial.reshape(GX, OWNED // 4, 2, LANES), GXS).reshape(MX * MY // 2, LANES)
     result = call(
         k7,
         jax.ShapeDtypeStruct((2, C, C * KZL, OWNED), F32),
@@ -426,21 +485,22 @@
         jnp.asarray(reorder_table()),
         spectral.reshape(2, C, C * KZL, OWNED),
         momentum.reshape(2, C, C * KZL, OWNED),
-        scratch=[pltpu.VMEM((2 * OWNED + 8, LANES), F32)],
+        scratch=[pltpu.VMEM((80, LANES), F32)],
     )
     result = result.reshape(2, C, C, KZL, OWNED)
     return jnp.transpose(result, (4, 0, 1, 2, 3))
 
 
 def solution(mesh):
+    chips = jax.sharding.Mesh(mesh.devices.reshape(GX // 2, 2, GY), ("chip", "core", "gy"))
     in_specs = (
-        P(None, "gx", "gy", None),
+        P(None, GXS, "gy", None),
         P(),
-        P("gx", None, None, None, "gy"),
-        P("gx", None, None, None, "gy"),
-        P(None, "gx", "gy", None),
-    )
-    out_specs = P("gx", None, None, None, "gy")
+        P(GXS, None, None, None, "gy"),
+        P(GXS, None, None, None, "gy"),
+        P(None, GXS, "gy", None),
+    )
+    out_specs = P(GXS, None, None, None, "gy")
     return jax.shard_map(
-        on_device, mesh=mesh, in_specs=in_specs, out_specs=out_specs, check_vma=False
-    )
+        on_device, mesh=chips, in_specs=in_specs, out_specs=out_specs, check_vma=False
+    )

time: 121 us -> 115 us (0.950)
  blocking collectives: 109 us -> 103 us
  local copies, waits for them, and re-layouts: 2.44 us -> 0.1 us
  Pallas kernels: 9.55 us -> 11.3 us
    all_to_all x6, blocking collectives: 109 us -> 103 us  [swap(): return lax.all_to_all(value, axis, split_axis=0, concat_axis=0, tiled=True)]
    unnamed x34, local copies, waits for them, and re-layouts: 2.44 us -> 0.1 us
    pallas_call x7, Pallas kernels: 9.55 us -> 11.3 us  [call(): pl.pallas_call(body, out_shape=out, in_specs=specs, out_specs=jax.tree.ma...]
where the time goes in v3:
time: 115 us; the launch traced here: 114 us
  blocking collectives  103 us (90%)
  Pallas kernels  11.3 us (10%)
    all_to_all x6, blocking collectives, swap(): return lax.all_to_all(value, axis, split_axis=0, concat_axis=0, tiled=True)  103 us
    pallas_call x7, Pallas kernels, call(): pl.pallas_call(body, out_shape=out, in_specs=specs, out_specs=jax.tree.ma...  11.3 us

profile of v3, /device:TPU:1, one launch (start us, length us, event | category | flops | bytes accessed | tf_op | source)
XLA Modules:
  0.0 114.4 jit_solution(12896503426887952855)
XLA Ops:
  0.0 0.0 copy-start.12
  0.0 2.5 %shard_map.172 = bf16[8,96,128]{2,1,0:T(8,128)(2,1)S(1)} custom-call(bf16[16,96,512]{2,1,0:T(8,128)(2,1)} %bitcast.19, bf16[1024,128]{1,0:T(8,128)(2,1)} %constant.26.clone.w_ref), custom_call_target="tpu_custom_call" | custom-call | tf_op jit(solution)/shard_map/pallas_call | solution.py:398
  2.6 0.0 copy-start.4
  2.6 0.0 copy-start.10
  2.6 16.3 %all_to_all.30.in_ref = bf16[8,96,128]{2,1,0:T(8,128)(2,1)S(1)} all-to-all(bf16[8,96,128]{2,1,0:T(8,128)(2,1)S(1)} %shard_map.172), channel_id=1, replica_groups=mesh['chip'=32,'core'=2,'gy'=8] {'gy'}, dimensions={0} | all-to-all | bytes 393216 | tf_op jit(solution)/shard_map/all_to_all | solution.py:409
  18.9 0.0 copy-start.5
  18.9 0.0 copy-start.6
  18.9 0.0 copy-start.15
  18.9 1.0 shard_map.173
  19.9 29.1 %all_to_all.31 = bf16[64,16,128]{2,1,0:T(8,128)(2,1)S(1)} all-to-all(bf16[64,16,128]{2,1,0:T(8,128)(2,1)S(1)} %bitcast.26), channel_id=1, replica_groups=mesh['chip'=32,'core'=2,'gy'=8] {'chip','core'}, dimensions={0} | all-to-all | bytes 524288 | tf_op jit(solution)/shard_map/all_to_all | solution.py:409
  49.0 1.1 shard_map.174
  50.1 14.6 %all_to_all.32 = bf16[64,4,128]{2,1,0:T(4,128)(2,1)S(1)} all-to-all(bf16[64,4,128]{2,1,0:T(4,128)(2,1)S(1)} %bitcast.30), channel_id=1, replica_groups=mesh['chip'=32,'core'=2,'gy'=8] {'chip','core'}, dimensions={0} | all-to-all | bytes 131072 | tf_op jit(solution)/shard_map/all_to_all | solution.py:409
  64.7 0.5 shard_map.175
  65.2 12.4 %all_to_all.33.waves_ref = bf16[8,96,128]{2,1,0:T(8,128)(2,1)S(1)} all-to-all(bf16[8,96,128]{2,1,0:T(8,128)(2,1)S(1)} %get-tuple-element.7), channel_id=1, replica_groups=mesh['chip'=32,'core'=2,'gy'=8] {'gy'}, dimensions={0} | all-to-all | bytes 393216 | tf_op jit(solution)/shard_map/all_to_all | solution.py:409
  77.6 0.0 copy-start.7
  77.7 0.0 copy-start.8
  77.7 0.0 copy-start.13
  77.7 0.0 copy-start.16
  77.7 2.9 %shard_map.176 = bf16[16,48,128]{2,1,0:T(8,128)(2,1)S(1)} custom-call(bf16[8,96,128]{2,1,0:T(8,128)(2,1)S(1)} %all_to_all.33.waves_ref, bf16[16,96,512]{2,1,0:T(8,128)(2,1)S(1)} %bitcast.20, bf16[16,96,512]{2,1,0:T(8,128)(2,1)S(1)} %bitcast.23, bf16[16,16]{1,0:T(8,128)(2,1)S(1)} %copy-done.15, bf16[1024,128]{1,0:T(8,128)(2,1)S(1)} %copy-done.6, ...), custom_call_target="tpu_custom_call" | custom-call | tf_op jit(solution)/shard_map/pallas_call | solution.py:398
  80.6 0.0 copy-start.14
  80.7 12.3 %all_to_all.34.in_ref = bf16[16,48,128]{2,1,0:T(8,128)(2,1)S(1)} all-to-all(bf16[16,48,128]{2,1,0:T(8,128)(2,1)S(1)} %shard_map.176), channel_id=1, replica_groups=mesh['chip'=32,'core'=2,'gy'=8] {'core','gy'}, dimensions={0} | all-to-all | bytes 393216 | tf_op jit(solution)/shard_map/all_to_all | solution.py:409
  93.0 1.6 %shard_map.177 = bf16[1152,128]{1,0:T(8,128)(2,1)S(1)} custom-call(bf16[16,48,128]{2,1,0:T(8,128)(2,1)S(1)} %all_to_all.34.in_ref, bf16[192,192]{1,0:T(8,128)(2,1)S(1)} %copy-done.13, f32[384,128]{1,0:T(8,128)S(1)} %copy-done.8, f32[384,128]{1,0:T(8,128)S(1)} %copy-done.7, f32[512]{0:T(512)S(1)} %copy-done.16), custom_call_target="tpu_custom_call" | custom-call | tf_op jit(solution)/shard_map/pallas_call | solution.py:398
  94.6 18.1 %all_to_all.35 = bf16[64,9,2,128]{3,2,1,0:T(2,128)(2,1)S(1)} all-to-all(bf16[64,9,2,128]{3,2,1,0:T(2,128)(2,1)S(1)} %bitcast.24), channel_id=1, replica_groups=mesh['chip'=32,'core'=2,'gy'=8] {'chip','core'}, dimensions={0} | all-to-all | bytes 589824 | tf_op jit(solution)/shard_map/all_to_all | solution.py:409
  112.6 1.8 %shard_map.178 = f32[2,16,64,36]{3,2,1,0:T(8,128)} custom-call(bf16[1152,128]{1,0:T(8,128)(2,1)S(1)} %bitcast.25, f32[48,128]{1,0:T(8,128)S(1)} %get-tuple-element.8.fwd_ref, bf16[128,128]{1,0:T(8,128)(2,1)S(1)} %copy-done.14, f32[2,16,64,36]{3,2,1,0:T(8,128)S(1)} %bitcast.22, f32[2,16,64,36]{3,2,1,0:T(8,128)S(1)} %bitcast.27), custom_call_target="tpu_custom_call" | custom-call | tf_op jit(solution)/shard_map/pallas_call | solution.py:398
  (23 shorter events, 0.0 us)
Async XLA Ops:
  0.0 18.9 %copy-start.11 = (bf16[192,192]{1,0:T(8,128)(2,1)S(1)}, bf16[192,192]{1,0:T(8,128)(2,1)}, u32[]{:S(2)}) copy-start(bf16[192,192]{1,0:T(8,128)(2,1)} %constant.29.clone.ty_ref) | copy-start | bytes 221188
  0.0 18.9 %copy-start.1 = (f32[36,2,16,16,4]{0,4,3,2,1:T(4,128)S(1)}, f32[36,2,16,16,4]{0,4,3,2,1:T(4,128)}, u32[]{:S(2)}) copy-start(f32[36,2,16,16,4]{0,4,3,2,1:T(4,128)} %param.20) | copy-start | bytes 884740
  0.0 49.0 %copy-start.9 = (bf16[256,192]{1,0:T(8,128)(2,1)S(1)}, bf16[256,192]{1,0:T(8,128)(2,1)}, u32[]{:S(2)}) copy-start(bf16[256,192]{1,0:T(8,128)(2,1)} %constant.32.clone.tinv_ref) | copy-start | bytes 294916
  0.0 64.7 %copy-start.12 = (bf16[192,192]{1,0:T(8,128)(2,1)S(1)}, bf16[192,192]{1,0:T(8,128)(2,1)}, u32[]{:S(2)}) copy-start(bf16[192,192]{1,0:T(8,128)(2,1)} %constant.33.clone.ty_ref) | copy-start | bytes 221188
  2.6 46.5 %copy-start.4 = (bf16[128,1536]{1,0:T(8,128)(2,1)S(1)}, bf16[128,1536]{1,0:T(8,128)(2,1)}, u32[]{:S(2)}) copy-start(bf16[128,1536]{1,0:T(8,128)(2,1)} %constant.31.clone.e_ref) | copy-start | bytes 1179652
  2.6 46.5 %copy-start.10 = (bf16[192,256]{1,0:T(8,128)(2,1)S(1)}, bf16[192,256]{1,0:T(8,128)(2,1)}, u32[]{:S(2)}) copy-start(bf16[192,256]{1,0:T(8,128)(2,1)} %constant.30.clone.tx_ref) | copy-start | bytes 294916
  18.9 58.7 %copy-start = (bf16[16,4,24,512]{3,2,1,0:T(8,128)(2,1)S(1)}, bf16[16,4,24,512]{3,2,1,0:T(8,128)(2,1)}, u32[]{:S(2)}) copy-start(bf16[16,4,24,512]{3,2,1,0:T(8,128)(2,1)} %param.18) | copy-start | bytes 4718596
  18.9 58.7 %copy-start.2 = (bf16[16,4,24,512]{3,2,1,0:T(8,128)(2,1)S(1)}, bf16[16,4,24,512]{3,2,1,0:T(8,128)(2,1)}, u32[]{:S(2)}) copy-start(bf16[16,4,24,512]{3,2,1,0:T(8,128)(2,1)} %param.22) | copy-start | bytes 4718596
  18.9 58.7 %copy-start.5 = (bf16[128,1024]{1,0:T(8,128)(2,1)S(1)}, bf16[128,1024]{1,0:T(8,128)(2,1)}, u32[]{:S(2)}) copy-start(bf16[128,1024]{1,0:T(8,128)(2,1)} %constant.28.clone.zt_ref) | copy-start | bytes 786436
  18.9 58.7 %copy-start.6 = (bf16[1024,128]{1,0:T(8,128)(2,1)S(1)}, bf16[1024,128]{1,0:T(8,128)(2,1)}, u32[]{:S(2)}) copy-start(bf16[1024,128]{1,0:T(8,128)(2,1)} %constant.27.clone.w_ref) | copy-start | bytes 786436
  18.9 58.7 %copy-start.15 = (bf16[16,16]{1,0:T(8,128)(2,1)S(1)}, bf16[16,16]{1,0:T(8,128)(2,1)}, u32[]{:S(2)}) copy-start(bf16[16,16]{1,0:T(8,128)(2,1)} %pw_ref.1) | copy-start | bytes 1540
  77.6 15.3 %copy-start.7 = (f32[384,128]{1,0:T(8,128)S(1)}, f32[384,128]{1,0:T(8,128)}, u32[]{:S(2)}) copy-start(f32[384,128]{1,0:T(8,128)} %constant.36.clone.turn_ref) | copy-start | bytes 589828
  77.7 15.3 %copy-start.8 = (f32[384,128]{1,0:T(8,128)S(1)}, f32[384,128]{1,0:T(8,128)}, u32[]{:S(2)}) copy-start(f32[384,128]{1,0:T(8,128)} %constant.35.clone.near_ref) | copy-start | bytes 589828
  77.7 15.3 %copy-start.13 = (bf16[192,192]{1,0:T(8,128)(2,1)S(1)}, bf16[192,192]{1,0:T(8,128)(2,1)}, u32[]{:S(2)}) copy-start(bf16[192,192]{1,0:T(8,128)(2,1)} %constant.34.clone.ty_ref) | copy-start | bytes 221188
  77.7 15.3 %copy-start.16 = (f32[512]{0:T(512)S(1)}, f32[512]{0:T(512)}, u32[]{:S(2)}) copy-start(f32[512]{0:T(512)} %constant.37.clone.cs_ref) | copy-start | bytes 6148
  80.6 32.0 %copy-start.3 = (f32[36,2,16,16,4]{0,4,3,2,1:T(4,128)S(1)}, f32[36,2,16,16,4]{0,4,3,2,1:T(4,128)}, u32[]{:S(2)}) copy-start(f32[36,2,16,16,4]{0,4,3,2,1:T(4,128)} %param.21) | copy-start | bytes 884740
  80.6 32.0 %copy-start.14 = (bf16[128,128]{1,0:T(8,128)(2,1)S(1)}, bf16[128,128]{1,0:T(8,128)(2,1)}, u32[]{:S(2)}) copy-start(bf16[128,128]{1,0:T(8,128)(2,1)} %constant.38.clone.reorder_ref) | copy-start | bytes 98308

commit v4 on v3

--- a/solution.py
+++ b/solution.py
@@ -85,9 +85,13 @@
     cos, sin = np.cos(a) / math.sqrt(NX), np.sin(a) / math.sqrt(NX)
     near = np.concatenate([cos, sin], 1).reshape(8 * MX, LANES)
     turn = np.concatenate([-sin, cos], 1).reshape(8 * MX, LANES)
-    whole = 2.0 * np.pi / NX * np.arange(NX)
-    whole = np.concatenate([np.cos(whole), np.sin(whole)])
-    return [t.astype(np.float32) for t in (near, turn, whole)]
+    eighth = 2.0 * np.pi / 32 * np.arange(32)
+    chip = np.repeat(np.stack([np.cos(eighth), np.sin(eighth)], 1), LANES, 1)
+    parts = []
+    for _ in range(3):
+        parts.append(chip.astype(ml_dtypes.bfloat16))
+        chip = chip - parts[-1].astype(np.float64)
+    return near.astype(np.float32), turn.astype(np.float32), np.concatenate(parts, 0)
 
 
 def expand_table():
@@ -161,7 +165,19 @@
     return [modes[i : i + ROWS] for i in range(0, modes.shape[0], ROWS)]
 
 
-def k1(field_ref, w_ref, out_ref, x_ref, t_ref, sems):
+def expand_pointwise(pw):
+    group = lax.broadcasted_iota(jnp.int32, (256, C), 0) // 16
+    member = lax.broadcasted_iota(jnp.int32, (256, C), 1)
+    one_hot = (group == member).astype(BF)
+    wide = dot_t(dot_t(one_hot, pw).astype(BF), one_hot)
+    r = lax.broadcasted_iota(jnp.int32, (256, 256), 0) % 16
+    s = lax.broadcasted_iota(jnp.int32, (256, 256), 1) % 16
+    return jnp.where(r == s, wide, 0.0).astype(BF)
+
+
+def k1(field_ref, w_ref, pw_ref, out_ref, kron_ref, x_ref, t_ref, p_ref, sems):
+    small = pltpu.make_async_copy(pw_ref, p_ref, sems.at[9])
+    small.start()
     table = pltpu.make_async_copy(w_ref, t_ref, sems.at[8])
     table.start()
     copies = []
@@ -170,6 +186,8 @@
             part = pl.ds(8 * h + 2 * n, 2)
             copies.append(pltpu.make_async_copy(field_ref.at[part], x_ref.at[part], sems.at[2 * n + h]))
             copies[-1].start()
+    small.wait()
+    kron_ref[...] = expand_pointwise(p_ref[...])
     table.wait()
     modes = []
     for n in range(4):
@@ -219,15 +237,31 @@
     out_ref[...] = scratch[...].astype(BF)
 
 
+def fold(arrays):
+    lane = lane_of(arrays[0].shape)
+    zero = jnp.zeros_like(arrays[0])
+    arrays = arrays + [zero, zero]
+    for stride in (64, 32, 16):
+        n = len(arrays) // 2
+        clear = (lane & stride) == 0
+        merged = []
+        for lo, hi in zip(arrays[:n], arrays[n:]):
+            moved = jnp.where(clear, hi, lo)
+            back = pltpu.roll(moved, stride, 1)
+            if stride < 64:
+                back = jnp.where(clear, pltpu.roll(moved, LANES - stride, 1), back)
+            merged.append(jnp.where(clear, lo, hi) + back)
+        arrays = merged
+    return arrays[0]
+
+
 def k3(in_ref, tx_ref, e_ref, tinv_ref, out_ref, scratch):
     a = place() // 4
     scratch[...] = in_ref[...].astype(F32)
     data = jnp.concatenate([scratch[pl.ds(x, GX, stride=16), :] for x in range(XL)], 0).astype(BF)
     t = dot(tx_ref[...], data)
     fwd = t[0:48] + t[48:96] + times_minus_i(t[96:144] + t[144:192], 16)
-    high = fwd.astype(BF)
-    low = (fwd - high.astype(F32)).astype(BF)
-    both = jnp.concatenate([high, low], 0)
+    fwd = fwd.astype(BF)
     source = (
         jnp.where(a >= 12, 1, 0),
         1 + jnp.where(a >= 8, 1, 0),
@@ -240,27 +274,22 @@
             [scratch[pl.ds(16 * source[r] + at, 16, stride=64), :] for r in range(3)], 0
         )
 
-    group = lane_of((MX, LANES)) // 16
-    mixed = jnp.zeros((MX, LANES), F32)
+    sums = []
     for i in range(3):
-        sums = [0.0, 0.0]
+        real, imag = 0.0, 0.0
         for h in range(2):
             at = 256 * (2 * i + h)
-            wide = dot(both, e_ref[:, at : at + 256])
-            wide = wide[0:48] + wide[48:96]
+            wide = dot(fwd, e_ref[:, at : at + 256])
             fr, fi = wide[:, 0:128], wide[:, 128:256]
             wr, wi = weights(i, h), weights(i, 2 + h)
-            sums[0] += wr * fr - wi * fi
-            sums[1] += wr * fi + wi * fr
-        for r in range(2):
-            v = sums[r]
-            for stride in (64, 32, 16):
-                v = v + pltpu.roll(v, stride, 1)
-            mixed = jnp.where(group == 2 * i + r, v, mixed)
+            real += wr * fr - wi * fi
+            imag += wr * fi + wi * fr
+        sums += [real, imag]
+    mixed = fold(sums)
     mixed = mixed.astype(BF)
     turned = times_plus_i(mixed.astype(F32), 16).astype(BF)
     moved = [
-        jnp.where(group >= 6, pltpu.roll(high.astype(F32), 96 - 32 * i, 1), 0.0)
+        jnp.where(lane_of(fwd.shape) >= 96, pltpu.roll(fwd.astype(F32), 96 - 32 * i, 1), 0.0)
         for i in range(3)
     ]
     moved = jnp.concatenate(moved, 0).astype(BF)
@@ -300,22 +329,15 @@
     return (0.5 + 0.5 * t) + (1.0 - t * t) * ramp
 
 
-def k5(waves_ref, field_ref, cot_ref, pw_ref, w_ref, zt_ref, out_ref, kron, grad):
-    group = lax.broadcasted_iota(jnp.int32, (256, C), 0) // 16
-    member = lax.broadcasted_iota(jnp.int32, (256, C), 1)
-    one_hot = (group == member).astype(BF)
-    wide = dot_t(dot_t(one_hot, pw_ref[...]).astype(BF), one_hot)
-    r = lax.broadcasted_iota(jnp.int32, (256, 256), 0) % 16
-    s = lax.broadcasted_iota(jnp.int32, (256, 256), 1) % 16
-    kron[...] = jnp.where(r == s, wide, 0.0).astype(BF)
+def k5(waves_ref, field_ref, cot_ref, kron, w_ref, zt_ref, out_ref, grad):
     for n in range(ROWS // 16):
         rows = slice(16 * n, 16 * n + 16)
         parts = exchange([waves_ref[p, rows, :].astype(F32) for p in range(GY)], 1)
         waves = jnp.concatenate(parts, 0).astype(BF)
         x = field_ref[:, rows, :].reshape(C * 16, NZ)
+        mapped = dot(kron[...], x)
         for h in range(2):
-            pre = dot(waves, zt_ref[:, NZ * h : NZ * h + NZ])
-            pre += dot(kron[128 * h : 128 * h + 128, :], x)
+            pre = dot(waves, zt_ref[:, NZ * h : NZ * h + NZ]) + mapped[128 * h : 128 * h + 128]
             cot = cot_ref[8 * h : 8 * h + 8, rows, :].reshape(128, NZ).astype(F32)
             grad[8 * h : 8 * h + 8, rows, :] = (cot * slope(pre)).astype(BF).reshape(8, 16, NZ)
     even = grad[0:8].reshape(8 * ROWS, NZ)
@@ -325,12 +347,15 @@
             out_ref[8 * core + p] = part.astype(BF)
 
 
-def k6(in_ref, ty_ref, near_ref, turn_ref, cs_ref, out_ref, factors):
-    chip = lax.axis_index("chip")
+def k6(in_ref, ty_ref, near_ref, turn_ref, chip_ref, out_ref, factors):
+    kx = lax.broadcasted_iota(jnp.int32, (MX, 96), 0)
+    member = lax.broadcasted_iota(jnp.int32, (MX, 96), 1) % 32
+    one_hot = (member == (kx * lax.axis_index("chip")) % 32).astype(BF)
+    chip = dot(one_hot, chip_ref[...])
     for kx in range(MX):
-        at = (8 * kx * chip) & (NX - 1)
         rows = slice(8 * kx, 8 * kx + 8)
-        factors[rows, :] = near_ref[rows, :] * cs_ref[at] + turn_ref[rows, :] * cs_ref[NX + at]
+        cos, sin = chip[kx : kx + 1, 0:128], chip[kx : kx + 1, 128:256]
+        factors[rows, :] = near_ref[rows, :] * cos + turn_ref[rows, :] * sin
     full = in_ref[...].astype(F32)
     values = []
     for core in range(2):
@@ -350,7 +375,7 @@
         out_ref[24 * kx : 24 * kx + 48, :] = jnp.concatenate(rows, 0).astype(BF)
 
 
-def k7(in_ref, fwd_ref, reorder_ref, spec_ref, mom_ref, out_ref, scratch):
+def k7(in_ref, fwd_ref, reorder_ref, spec_ref, mom_ref, out_ref, scratch, result, sems):
     quarter = place() % 4
     total = in_ref[0:72, :].astype(F32)
     for g in range(1, 16):
@@ -358,11 +383,15 @@
     scratch[0:72, :] = total
     scratch[72:80, :] = jnp.zeros((8, LANES), F32)
     total = scratch[0:40, :] + scratch[36:76, :]
-    row = lax.broadcasted_iota(jnp.int32, (2 * LANES, 40), 0)
-    col = lax.broadcasted_iota(jnp.int32, (2 * LANES, 40), 1)
+    row = lax.broadcasted_iota(jnp.int32, (2 * LANES, 120), 0)
+    col = lax.broadcasted_iota(jnp.int32, (2 * LANES, 120), 1) % 40
     mode = row % LANES
-    select = ((col == 18 * (row // LANES) + mode // 2) & (mode < OWNED)).astype(F32)
-    moved = jnp.dot(select, total, precision=lax.Precision.HIGHEST, preferred_element_type=F32)
+    select = ((col == 18 * (row // LANES) + mode // 2) & (mode < OWNED)).astype(BF)
+    parts = []
+    for _ in range(3):
+        parts.append(total.astype(BF).astype(F32))
+        total = total - parts[-1]
+    moved = dot(select, jnp.concatenate(parts, 0).astype(BF))
     first, second = moved[0:LANES], moved[LANES : 2 * LANES]
     odd = lax.broadcasted_iota(jnp.int32, (LANES, LANES), 0) % 2
     upper = lane_of((LANES, LANES)) // 64
@@ -378,6 +407,7 @@
     fwd = fwd.T[:, 0:OWNED]
     grad_r = jnp.concatenate([grads[0:32], grads[64:96]], 0)
     grad_i = jnp.concatenate([grads[32:64], grads[96:128]], 0)
+    copies = []
     for c in range(C):
         fr = fwd[4 * c : 4 * c + 4]
         fi = fwd[64 + 4 * c : 68 + 4 * c]
@@ -385,21 +415,30 @@
         fi = jnp.concatenate([fi] * 16, 0)
         d_real = grad_r * fr + grad_i * fi
         d_imag = grad_i * fr - grad_r * fi
-        out_ref[0, c] = mom_ref[0, c] - 0.25 * (d_real + 2.0 * C * spec_ref[0, c])
-        out_ref[1, c] = mom_ref[1, c] - 0.25 * (d_imag + 2.0 * C * spec_ref[1, c])
-
-
-def call(body, out, *args, scratch=(), smem=(), hbm=()):
+        result[0, c] = mom_ref[0, c] - 0.25 * (d_real + 2.0 * C * spec_ref[0, c])
+        result[1, c] = mom_ref[1, c] - 0.25 * (d_imag + 2.0 * C * spec_ref[1, c])
+        if c % 4 == 3:
+            for r in range(2):
+                part = pl.ds(c - 3, 4)
+                copy = pltpu.make_async_copy(
+                    result.at[r, part], out_ref.at[r, part], sems.at[2 * (c // 4) + r]
+                )
+                copy.start()
+                copies.append(copy)
+    for copy in copies:
+        copy.wait()
+
+
+def call(body, out, *args, scratch=(), hbm=(), out_space=pltpu.VMEM):
     specs = [
-        pl.BlockSpec(memory_space=pltpu.SMEM if i in smem else pltpu.HBM if i in hbm else pltpu.VMEM)
-        for i in range(len(args))
+        pl.BlockSpec(memory_space=pltpu.HBM if i in hbm else pltpu.VMEM) for i in range(len(args))
     ]
-    vmem = pl.BlockSpec(memory_space=pltpu.VMEM)
+    out_spec = pl.BlockSpec(memory_space=out_space)
     return pl.pallas_call(
         body,
         out_shape=out,
         in_specs=specs,
-        out_specs=jax.tree.map(lambda _: vmem, out),
+        out_specs=jax.tree.map(lambda _: out_spec, out),
         scratch_shapes=list(scratch),
         compiler_params=pltpu.CompilerParams(vmem_limit_bytes=40 * 1024 * 1024),
     )(*args)
@@ -417,16 +456,18 @@
     z_mid, z_half, z_inv = [jnp.asarray(t) for t in z_tables()]
     zshape = jax.ShapeDtypeStruct((GY, ROWS, LANES), BF)
 
-    zmodes = call(
+    zmodes, kron = call(
         k1,
-        zshape,
+        (zshape, jax.ShapeDtypeStruct((256, 256), BF)),
         pltpu.with_memory_space_constraint(field, pltpu.HBM),
         pltpu.with_memory_space_constraint(z_mid, pltpu.HBM),
-        hbm=(0, 1),
+        pltpu.with_memory_space_constraint(pointwise, pltpu.HBM),
+        hbm=(0, 1, 2),
         scratch=[
             pltpu.VMEM((C, ROWS, NZ), BF),
             pltpu.VMEM((2 * NZ, LANES), BF),
-            pltpu.SemaphoreType.DMA((9,)),
+            pltpu.VMEM((C, C), BF),
+            pltpu.SemaphoreType.DMA((10,)),
         ],
     )
     zmodes = swap(zmodes, "gy")
@@ -462,10 +503,10 @@
         swap(waves, "gy"),
         field,
         cotangent,
-        pointwise,
+        kron,
         z_half,
         z_inv,
-        scratch=[pltpu.VMEM((256, 256), BF), pltpu.VMEM((C, ROWS, NZ), BF)],
+        scratch=[pltpu.VMEM((C, ROWS, NZ), BF)],
     )
     partial = call(
         k6,
@@ -473,7 +514,6 @@
         swap(zgrads, ("core", "gy")),
         jnp.asarray(y_forward_table(PAIRS)),
         *[jnp.asarray(t) for t in partial_tables()],
-        smem=(4,),
         scratch=[pltpu.VMEM((8 * MX, LANES), F32)],
     )
     partial = swap(partial.reshape(GX, OWNED // 4, 2, LANES), GXS).reshape(MX * MY // 2, LANES)
@@ -485,7 +525,12 @@
         jnp.asarray(reorder_table()),
         spectral.reshape(2, C, C * KZL, OWNED),
         momentum.reshape(2, C, C * KZL, OWNED),
-        scratch=[pltpu.VMEM((80, LANES), F32)],
+        scratch=[
+            pltpu.VMEM((80, LANES), F32),
+            pltpu.VMEM((2, C, C * KZL, OWNED), F32),
+            pltpu.SemaphoreType.DMA((8,)),
+        ],
+        out_space=pltpu.HBM,
     )
     result = result.reshape(2, C, C, KZL, OWNED)
     return jnp.transpose(result, (4, 0, 1, 2, 3))

time: 115 us -> 114 us (level)
  no operation moved by 1% of the time
where the time goes in v4:
time: 114 us
  blocking collectives  103 us (90%)
  Pallas kernels  10.5 us (9%)
    all_to_all x6, blocking collectives, swap(): return lax.all_to_all(value, axis, split_axis=0, concat_axis=0, tiled=True)  103 us
    pallas_call x7, Pallas kernels, call(): pl.pallas_call(body, out_shape=out, in_specs=specs, out_specs=jax.tree.ma...  10.5 us

profile of v4, /device:TPU:1, one launch (start us, length us, event | category | flops | bytes accessed | tf_op | source)
XLA Modules:
  0.0 113.5 jit_solution(7157950854754842475)
XLA Ops:
  0.0 0.0 copy-start.12
  0.0 2.6 %shard_map.172 = (bf16[8,96,128]{2,1,0:T(8,128)(2,1)S(1)}, bf16[256,256]{1,0:T(8,128)(2,1)S(1)}) custom-call(bf16[16,96,512]{2,1,0:T(8,128)(2,1)} %bitcast.19, bf16[1024,128]{1,0:T(8,128)(2,1)} %constant.26.clone.w_ref, bf16[16,16]{1,0:T(8,128)(2,1)} %pw_ref.1), custom_call_target="tpu_custom_call" | custom-call | tf_op jit(solution)/shard_map/pallas_call | solution.py:437
  2.6 0.0 copy-start.4
  2.6 0.0 copy-start.10
  2.7 16.3 %all_to_all.30.in_ref = bf16[8,96,128]{2,1,0:T(8,128)(2,1)S(1)} all-to-all(bf16[8,96,128]{2,1,0:T(8,128)(2,1)S(1)} %get-tuple-element.9), channel_id=1, replica_groups=mesh['chip'=32,'core'=2,'gy'=8] {'gy'}, dimensions={0} | all-to-all | bytes 393216 | tf_op jit(solution)/shard_map/all_to_all | solution.py:448
  19.0 0.0 copy-start.5
  19.0 0.0 copy-start.6
  19.0 1.0 shard_map.173
  20.0 29.1 %all_to_all.31 = bf16[64,16,128]{2,1,0:T(8,128)(2,1)S(1)} all-to-all(bf16[64,16,128]{2,1,0:T(8,128)(2,1)S(1)} %bitcast.26), channel_id=1, replica_groups=mesh['chip'=32,'core'=2,'gy'=8] {'chip','core'}, dimensions={0} | all-to-all | bytes 524288 | tf_op jit(solution)/shard_map/all_to_all | solution.py:448
  49.1 1.0 shard_map.174
  50.1 14.6 %all_to_all.32 = bf16[64,4,128]{2,1,0:T(4,128)(2,1)S(1)} all-to-all(bf16[64,4,128]{2,1,0:T(4,128)(2,1)S(1)} %bitcast.30), channel_id=1, replica_groups=mesh['chip'=32,'core'=2,'gy'=8] {'chip','core'}, dimensions={0} | all-to-all | bytes 131072 | tf_op jit(solution)/shard_map/all_to_all | solution.py:448
  64.7 0.5 shard_map.175
  65.3 12.4 %all_to_all.33.waves_ref = bf16[8,96,128]{2,1,0:T(8,128)(2,1)S(1)} all-to-all(bf16[8,96,128]{2,1,0:T(8,128)(2,1)S(1)} %get-tuple-element.10), channel_id=1, replica_groups=mesh['chip'=32,'core'=2,'gy'=8] {'gy'}, dimensions={0} | all-to-all | bytes 393216 | tf_op jit(solution)/shard_map/all_to_all | solution.py:448
  77.6 0.0 copy-start.7
  77.7 0.0 copy-start.8
  77.7 0.0 copy-start.13
  77.7 0.0 copy-start.14
  77.7 2.8 %shard_map.176 = bf16[16,48,128]{2,1,0:T(8,128)(2,1)S(1)} custom-call(bf16[8,96,128]{2,1,0:T(8,128)(2,1)S(1)} %all_to_all.33.waves_ref, bf16[16,96,512]{2,1,0:T(8,128)(2,1)S(1)} %bitcast.20, bf16[16,96,512]{2,1,0:T(8,128)(2,1)S(1)} %bitcast.23, bf16[256,256]{1,0:T(8,128)(2,1)S(1)} %get-tuple-element.11.kron, bf16[1024,128]{1,0:T(8,128)(2,1)S(1)} %copy-done.6, ...), custom_call_target="tpu_custom_call" | custom-call | tf_op jit(solution)/shard_map/pallas_call | solution.py:437
  80.5 0.0 copy-start.3
  80.5 0.0 copy-start.15
  80.5 12.3 %all_to_all.34.in_ref = bf16[16,48,128]{2,1,0:T(8,128)(2,1)S(1)} all-to-all(bf16[16,48,128]{2,1,0:T(8,128)(2,1)S(1)} %shard_map.176), channel_id=1, replica_groups=mesh['chip'=32,'core'=2,'gy'=8] {'core','gy'}, dimensions={0} | all-to-all | bytes 393216 | tf_op jit(solution)/shard_map/all_to_all | solution.py:448
  92.8 1.0 shard_map.177
  93.9 18.1 %all_to_all.35 = bf16[64,9,2,128]{3,2,1,0:T(2,128)(2,1)S(1)} all-to-all(bf16[64,9,2,128]{3,2,1,0:T(2,128)(2,1)S(1)} %bitcast.24), channel_id=1, replica_groups=mesh['chip'=32,'core'=2,'gy'=8] {'chip','core'}, dimensions={0} | all-to-all | bytes 589824 | tf_op jit(solution)/shard_map/all_to_all | solution.py:448
  111.9 1.6 %shard_map.178 = f32[2,16,64,36]{3,2,1,0:T(8,128)} custom-call(bf16[1152,128]{1,0:T(8,128)(2,1)S(1)} %bitcast.25, f32[48,128]{1,0:T(8,128)S(1)} %get-tuple-element.12.fwd_ref, bf16[128,128]{1,0:T(8,128)(2,1)S(1)} %copy-done.15, f32[2,16,64,36]{3,2,1,0:T(8,128)S(1)} %bitcast.22, f32[2,16,64,36]{3,2,1,0:T(8,128)S(1)} %bitcast.27), custom_call_target="tpu_custom_call" | custom-call | tf_op jit(solution)/shard_map/pallas_call | solution.py:437
  (21 shorter events, 0.0 us)
Async XLA Ops:
  0.0 19.0 %copy-start.11 = (bf16[192,192]{1,0:T(8,128)(2,1)S(1)}, bf16[192,192]{1,0:T(8,128)(2,1)}, u32[]{:S(2)}) copy-start(bf16[192,192]{1,0:T(8,128)(2,1)} %constant.29.clone.ty_ref) | copy-start | bytes 221188
  0.0 19.0 %copy-start.1 = (f32[36,2,16,16,4]{0,4,3,2,1:T(4,128)S(1)}, f32[36,2,16,16,4]{0,4,3,2,1:T(4,128)}, u32[]{:S(2)}) copy-start(f32[36,2,16,16,4]{0,4,3,2,1:T(4,128)} %param.20) | copy-start | bytes 884740
  0.0 49.1 %copy-start.9 = (bf16[256,192]{1,0:T(8,128)(2,1)S(1)}, bf16[256,192]{1,0:T(8,128)(2,1)}, u32[]{:S(2)}) copy-start(bf16[256,192]{1,0:T(8,128)(2,1)} %constant.32.clone.tinv_ref) | copy-start | bytes 294916
  0.0 64.7 %copy-start.12 = (bf16[192,192]{1,0:T(8,128)(2,1)S(1)}, bf16[192,192]{1,0:T(8,128)(2,1)}, u32[]{:S(2)}) copy-start(bf16[192,192]{1,0:T(8,128)(2,1)} %constant.33.clone.ty_ref) | copy-start | bytes 221188
  2.6 46.5 %copy-start.4 = (bf16[128,1536]{1,0:T(8,128)(2,1)S(1)}, bf16[128,1536]{1,0:T(8,128)(2,1)}, u32[]{:S(2)}) copy-start(bf16[128,1536]{1,0:T(8,128)(2,1)} %constant.31.clone.e_ref) | copy-start | bytes 1179652
  2.6 46.5 %copy-start.10 = (bf16[192,256]{1,0:T(8,128)(2,1)S(1)}, bf16[192,256]{1,0:T(8,128)(2,1)}, u32[]{:S(2)}) copy-start(bf16[192,256]{1,0:T(8,128)(2,1)} %constant.30.clone.tx_ref) | copy-start | bytes 294916
  19.0 58.6 %copy-start = (bf16[16,4,24,512]{3,2,1,0:T(8,128)(2,1)S(1)}, bf16[16,4,24,512]{3,2,1,0:T(8,128)(2,1)}, u32[]{:S(2)}) copy-start(bf16[16,4,24,512]{3,2,1,0:T(8,128)(2,1)} %param.18) | copy-start | bytes 4718596
  19.0 58.6 %copy-start.2 = (bf16[16,4,24,512]{3,2,1,0:T(8,128)(2,1)S(1)}, bf16[16,4,24,512]{3,2,1,0:T(8,128)(2,1)}, u32[]{:S(2)}) copy-start(bf16[16,4,24,512]{3,2,1,0:T(8,128)(2,1)} %param.22) | copy-start | bytes 4718596
  19.0 58.6 %copy-start.5 = (bf16[128,1024]{1,0:T(8,128)(2,1)S(1)}, bf16[128,1024]{1,0:T(8,128)(2,1)}, u32[]{:S(2)}) copy-start(bf16[128,1024]{1,0:T(8,128)(2,1)} %constant.28.clone.zt_ref) | copy-start | bytes 786436
  19.0 58.6 %copy-start.6 = (bf16[1024,128]{1,0:T(8,128)(2,1)S(1)}, bf16[1024,128]{1,0:T(8,128)(2,1)}, u32[]{:S(2)}) copy-start(bf16[1024,128]{1,0:T(8,128)(2,1)} %constant.27.clone.w_ref) | copy-start | bytes 786436
  77.6 15.2 %copy-start.7 = (f32[384,128]{1,0:T(8,128)S(1)}, f32[384,128]{1,0:T(8,128)}, u32[]{:S(2)}) copy-start(f32[384,128]{1,0:T(8,128)} %constant.36.clone.turn_ref) | copy-start | bytes 589828
  77.7 15.2 %copy-start.8 = (f32[384,128]{1,0:T(8,128)S(1)}, f32[384,128]{1,0:T(8,128)}, u32[]{:S(2)}) copy-start(f32[384,128]{1,0:T(8,128)} %constant.35.clone.near_ref) | copy-start | bytes 589828
  77.7 15.1 %copy-start.13 = (bf16[192,192]{1,0:T(8,128)(2,1)S(1)}, bf16[192,192]{1,0:T(8,128)(2,1)}, u32[]{:S(2)}) copy-start(bf16[192,192]{1,0:T(8,128)(2,1)} %constant.34.clone.ty_ref) | copy-start | bytes 221188
  77.7 15.1 %copy-start.14 = (bf16[96,256]{1,0:T(8,128)(2,1)S(1)}, bf16[96,256]{1,0:T(8,128)(2,1)}, u32[]{:S(2)}) copy-start(bf16[96,256]{1,0:T(8,128)(2,1)} %constant.37.clone.chip_ref) | copy-start | bytes 147460
  80.5 31.5 %copy-start.3 = (f32[36,2,16,16,4]{0,4,3,2,1:T(4,128)S(1)}, f32[36,2,16,16,4]{0,4,3,2,1:T(4,128)}, u32[]{:S(2)}) copy-start(f32[36,2,16,16,4]{0,4,3,2,1:T(4,128)} %param.21) | copy-start | bytes 884740
  80.5 31.5 %copy-start.15 = (bf16[128,128]{1,0:T(8,128)(2,1)S(1)}, bf16[128,128]{1,0:T(8,128)(2,1)}, u32[]{:S(2)}) copy-start(bf16[128,128]{1,0:T(8,128)(2,1)} %constant.38.clone.reorder_ref) | copy-start | bytes 98308

commit v5 on v4

--- a/solution.py
+++ b/solution.py
@@ -220,20 +220,20 @@
 
 
 def k2(in_ref, spec_ref, ty_ref, out_ref, scratch):
+    for x, v in enumerate(y_transform(in_ref[...].astype(F32), ty_ref, 16)):
+        parts = [v[0:16], v[16:32], v[32:48], jnp.zeros((16, LANES), F32)]
+        for b, part in enumerate(exchange(parts, 32)):
+            scratch[pl.ds(16 * b + x, 16, stride=64), :] = part
     quarter = place() % 4
     row = lax.broadcasted_iota(jnp.int32, (MY, OWNED), 0)
     mode = ky_of(lax.broadcasted_iota(jnp.int32, (MY, OWNED), 1), quarter)
     select = (mode == 3 * (row % 16) + row // 16).astype(BF)
-    for k in range(4):
-        for b in range(KZL):
-            block = spec_ref[pl.ds(512 * k + b, LANES, stride=KZL), :].astype(BF)
-            moved = dot_t(select, block)
+    for b in range(KZL):
+        moved = dot_t(select, spec_ref[pl.ds(b, 4 * LANES, stride=KZL), :].astype(BF))
+        for k in range(4):
             for i in range(3):
-                scratch[pl.ds(16 * b + 4 + 4 * i + k, 16, stride=64), :] = moved[16 * i : 16 * i + 16]
-    for x, v in enumerate(y_transform(in_ref[...].astype(F32), ty_ref, 16)):
-        parts = [v[0:16], v[16:32], v[32:48], jnp.zeros((16, LANES), F32)]
-        for b, part in enumerate(exchange(parts, 32)):
-            scratch[pl.ds(16 * b + x, 16, stride=64), :] = part
+                part = moved[16 * i : 16 * i + 16, LANES * k : LANES * k + LANES]
+                scratch[pl.ds(16 * b + 4 + 4 * i + k, 16, stride=64), :] = part
     out_ref[...] = scratch[...].astype(BF)
 
 

time: 114 us -> 114 us (level)
  no operation moved by 1% of the time
where the time goes in v5:
time: 114 us; the launch traced here: 113 us
  blocking collectives  103 us (90%)
  Pallas kernels  10.3 us (9%)
    all_to_all x6, blocking collectives, swap(): return lax.all_to_all(value, axis, split_axis=0, concat_axis=0, tiled=True)  103 us
    pallas_call x7, Pallas kernels, call(): pl.pallas_call(body, out_shape=out, in_specs=specs, out_specs=jax.tree.ma...  10.3 us

profile of v5, /device:TPU:1, one launch (start us, length us, event | category | flops | bytes accessed | tf_op | source)
XLA Modules:
  0.0 113.3 jit_solution(9554643921769165674)
XLA Ops:
  0.0 0.0 copy-start.12
  0.0 2.6 %shard_map.172 = (bf16[8,96,128]{2,1,0:T(8,128)(2,1)S(1)}, bf16[256,256]{1,0:T(8,128)(2,1)S(1)}) custom-call(bf16[16,96,512]{2,1,0:T(8,128)(2,1)} %bitcast.19, bf16[1024,128]{1,0:T(8,128)(2,1)} %constant.26.clone.w_ref, bf16[16,16]{1,0:T(8,128)(2,1)} %pw_ref.1), custom_call_target="tpu_custom_call" | custom-call | tf_op jit(solution)/shard_map/pallas_call | solution.py:437
  2.6 0.0 copy-start.4
  2.6 0.0 copy-start.10
  2.7 16.3 %all_to_all.30.in_ref = bf16[8,96,128]{2,1,0:T(8,128)(2,1)S(1)} all-to-all(bf16[8,96,128]{2,1,0:T(8,128)(2,1)S(1)} %get-tuple-element.9), channel_id=1, replica_groups=mesh['chip'=32,'core'=2,'gy'=8] {'gy'}, dimensions={0} | all-to-all | bytes 393216 | tf_op jit(solution)/shard_map/all_to_all | solution.py:448
  19.0 0.0 copy-start.5
  19.0 0.0 copy-start.6
  19.0 0.7 shard_map.173
  19.7 29.1 %all_to_all.31 = bf16[64,16,128]{2,1,0:T(8,128)(2,1)S(1)} all-to-all(bf16[64,16,128]{2,1,0:T(8,128)(2,1)S(1)} %bitcast.26), channel_id=1, replica_groups=mesh['chip'=32,'core'=2,'gy'=8] {'chip','core'}, dimensions={0} | all-to-all | bytes 524288 | tf_op jit(solution)/shard_map/all_to_all | solution.py:448
  48.9 1.0 shard_map.174
  49.9 14.6 %all_to_all.32 = bf16[64,4,128]{2,1,0:T(4,128)(2,1)S(1)} all-to-all(bf16[64,4,128]{2,1,0:T(4,128)(2,1)S(1)} %bitcast.30), channel_id=1, replica_groups=mesh['chip'=32,'core'=2,'gy'=8] {'chip','core'}, dimensions={0} | all-to-all | bytes 131072 | tf_op jit(solution)/shard_map/all_to_all | solution.py:448
  64.5 0.5 shard_map.175
  65.0 12.4 %all_to_all.33.waves_ref = bf16[8,96,128]{2,1,0:T(8,128)(2,1)S(1)} all-to-all(bf16[8,96,128]{2,1,0:T(8,128)(2,1)S(1)} %get-tuple-element.10), channel_id=1, replica_groups=mesh['chip'=32,'core'=2,'gy'=8] {'gy'}, dimensions={0} | all-to-all | bytes 393216 | tf_op jit(solution)/shard_map/all_to_all | solution.py:448
  77.4 0.0 copy-start.7
  77.4 0.0 copy-start.8
  77.4 0.0 copy-start.13
  77.4 0.0 copy-start.14
  77.5 2.8 %shard_map.176 = bf16[16,48,128]{2,1,0:T(8,128)(2,1)S(1)} custom-call(bf16[8,96,128]{2,1,0:T(8,128)(2,1)S(1)} %all_to_all.33.waves_ref, bf16[16,96,512]{2,1,0:T(8,128)(2,1)S(1)} %bitcast.20, bf16[16,96,512]{2,1,0:T(8,128)(2,1)S(1)} %bitcast.23, bf16[256,256]{1,0:T(8,128)(2,1)S(1)} %get-tuple-element.11.kron, bf16[1024,128]{1,0:T(8,128)(2,1)S(1)} %copy-done.6, ...), custom_call_target="tpu_custom_call" | custom-call | tf_op jit(solution)/shard_map/pallas_call | solution.py:437
  80.2 0.0 copy-start.3
  80.2 0.0 copy-start.15
  80.2 12.3 %all_to_all.34.in_ref = bf16[16,48,128]{2,1,0:T(8,128)(2,1)S(1)} all-to-all(bf16[16,48,128]{2,1,0:T(8,128)(2,1)S(1)} %shard_map.176), channel_id=1, replica_groups=mesh['chip'=32,'core'=2,'gy'=8] {'core','gy'}, dimensions={0} | all-to-all | bytes 393216 | tf_op jit(solution)/shard_map/all_to_all | solution.py:448
  92.6 1.0 shard_map.177
  93.6 18.1 %all_to_all.35 = bf16[64,9,2,128]{3,2,1,0:T(2,128)(2,1)S(1)} all-to-all(bf16[64,9,2,128]{3,2,1,0:T(2,128)(2,1)S(1)} %bitcast.24), channel_id=1, replica_groups=mesh['chip'=32,'core'=2,'gy'=8] {'chip','core'}, dimensions={0} | all-to-all | bytes 589824 | tf_op jit(solution)/shard_map/all_to_all | solution.py:448
  111.7 1.6 %shard_map.178 = f32[2,16,64,36]{3,2,1,0:T(8,128)} custom-call(bf16[1152,128]{1,0:T(8,128)(2,1)S(1)} %bitcast.25, f32[48,128]{1,0:T(8,128)S(1)} %get-tuple-element.12.fwd_ref, bf16[128,128]{1,0:T(8,128)(2,1)S(1)} %copy-done.15, f32[2,16,64,36]{3,2,1,0:T(8,128)S(1)} %bitcast.22, f32[2,16,64,36]{3,2,1,0:T(8,128)S(1)} %bitcast.27), custom_call_target="tpu_custom_call" | custom-call | tf_op jit(solution)/shard_map/pallas_call | solution.py:437
  (21 shorter events, 0.0 us)
Async XLA Ops:
  0.0 19.0 %copy-start.11 = (bf16[192,192]{1,0:T(8,128)(2,1)S(1)}, bf16[192,192]{1,0:T(8,128)(2,1)}, u32[]{:S(2)}) copy-start(bf16[192,192]{1,0:T(8,128)(2,1)} %constant.29.clone.ty_ref) | copy-start | bytes 221188
  0.0 19.0 %copy-start.1 = (f32[36,2,16,16,4]{0,4,3,2,1:T(4,128)S(1)}, f32[36,2,16,16,4]{0,4,3,2,1:T(4,128)}, u32[]{:S(2)}) copy-start(f32[36,2,16,16,4]{0,4,3,2,1:T(4,128)} %param.20) | copy-start | bytes 884740
  0.0 48.9 %copy-start.9 = (bf16[256,192]{1,0:T(8,128)(2,1)S(1)}, bf16[256,192]{1,0:T(8,128)(2,1)}, u32[]{:S(2)}) copy-start(bf16[256,192]{1,0:T(8,128)(2,1)} %constant.32.clone.tinv_ref) | copy-start | bytes 294916
  0.0 64.5 %copy-start.12 = (bf16[192,192]{1,0:T(8,128)(2,1)S(1)}, bf16[192,192]{1,0:T(8,128)(2,1)}, u32[]{:S(2)}) copy-start(bf16[192,192]{1,0:T(8,128)(2,1)} %constant.33.clone.ty_ref) | copy-start | bytes 221188
  2.6 46.2 %copy-start.4 = (bf16[128,1536]{1,0:T(8,128)(2,1)S(1)}, bf16[128,1536]{1,0:T(8,128)(2,1)}, u32[]{:S(2)}) copy-start(bf16[128,1536]{1,0:T(8,128)(2,1)} %constant.31.clone.e_ref) | copy-start | bytes 1179652
  2.6 46.2 %copy-start.10 = (bf16[192,256]{1,0:T(8,128)(2,1)S(1)}, bf16[192,256]{1,0:T(8,128)(2,1)}, u32[]{:S(2)}) copy-start(bf16[192,256]{1,0:T(8,128)(2,1)} %constant.30.clone.tx_ref) | copy-start | bytes 294916
  19.0 58.4 %copy-start = (bf16[16,4,24,512]{3,2,1,0:T(8,128)(2,1)S(1)}, bf16[16,4,24,512]{3,2,1,0:T(8,128)(2,1)}, u32[]{:S(2)}) copy-start(bf16[16,4,24,512]{3,2,1,0:T(8,128)(2,1)} %param.18) | copy-start | bytes 4718596
  19.0 58.4 %copy-start.2 = (bf16[16,4,24,512]{3,2,1,0:T(8,128)(2,1)S(1)}, bf16[16,4,24,512]{3,2,1,0:T(8,128)(2,1)}, u32[]{:S(2)}) copy-start(bf16[16,4,24,512]{3,2,1,0:T(8,128)(2,1)} %param.22) | copy-start | bytes 4718596
  19.0 58.4 %copy-start.5 = (bf16[128,1024]{1,0:T(8,128)(2,1)S(1)}, bf16[128,1024]{1,0:T(8,128)(2,1)}, u32[]{:S(2)}) copy-start(bf16[128,1024]{1,0:T(8,128)(2,1)} %constant.28.clone.zt_ref) | copy-start | bytes 786436
  19.0 58.4 %copy-start.6 = (bf16[1024,128]{1,0:T(8,128)(2,1)S(1)}, bf16[1024,128]{1,0:T(8,128)(2,1)}, u32[]{:S(2)}) copy-start(bf16[1024,128]{1,0:T(8,128)(2,1)} %constant.27.clone.w_ref) | copy-start | bytes 786436
  77.4 15.2 %copy-start.7 = (f32[384,128]{1,0:T(8,128)S(1)}, f32[384,128]{1,0:T(8,128)}, u32[]{:S(2)}) copy-start(f32[384,128]{1,0:T(8,128)} %constant.36.clone.turn_ref) | copy-start | bytes 589828
  77.4 15.2 %copy-start.8 = (f32[384,128]{1,0:T(8,128)S(1)}, f32[384,128]{1,0:T(8,128)}, u32[]{:S(2)}) copy-start(f32[384,128]{1,0:T(8,128)} %constant.35.clone.near_ref) | copy-start | bytes 589828
  77.4 15.1 %copy-start.13 = (bf16[192,192]{1,0:T(8,128)(2,1)S(1)}, bf16[192,192]{1,0:T(8,128)(2,1)}, u32[]{:S(2)}) copy-start(bf16[192,192]{1,0:T(8,128)(2,1)} %constant.34.clone.ty_ref) | copy-start | bytes 221188
  77.4 15.1 %copy-start.14 = (bf16[96,256]{1,0:T(8,128)(2,1)S(1)}, bf16[96,256]{1,0:T(8,128)(2,1)}, u32[]{:S(2)}) copy-start(bf16[96,256]{1,0:T(8,128)(2,1)} %constant.37.clone.chip_ref) | copy-start | bytes 147460
  80.2 31.5 %copy-start.3 = (f32[36,2,16,16,4]{0,4,3,2,1:T(4,128)S(1)}, f32[36,2,16,16,4]{0,4,3,2,1:T(4,128)}, u32[]{:S(2)}) copy-start(f32[36,2,16,16,4]{0,4,3,2,1:T(4,128)} %param.21) | copy-start | bytes 884740
  80.2 31.5 %copy-start.15 = (bf16[128,128]{1,0:T(8,128)(2,1)S(1)}, bf16[128,128]{1,0:T(8,128)(2,1)}, u32[]{:S(2)}) copy-start(bf16[128,128]{1,0:T(8,128)(2,1)} %constant.38.clone.reorder_ref) | copy-start | bytes 98308

commit v6 on v5

--- a/solution.py
+++ b/solution.py
@@ -27,6 +27,8 @@
 LANES = 128
 OWNED = MX * MY // GX
 GXS = ("chip", "core")
+CORE_FIRST = ("core", "chip")
+ORDER = np.arange(GX).reshape(GX // 2, 2).T.reshape(GX)
 TRIPLES = np.arange(48).reshape(16, 3).T.reshape(48)
 PAIRS = np.arange(48).reshape(24, 2).T.reshape(48)
 
@@ -62,13 +64,13 @@
 
 
 def x_forward_table():
-    xs = np.arange(NX).reshape(GX, XL).T.reshape(NX)
+    xs = np.arange(NX).reshape(GX, XL)[ORDER].T.reshape(NX)
     a = angle(TRIPLES, xs, NX)
     return np.concatenate(split(np.cos(a) / math.sqrt(NX)) + split(np.sin(a) / math.sqrt(NX)), 0)
 
 
 def x_inverse_table():
-    a = angle(np.arange(NX), TRIPLES, NX)
+    a = angle(np.arange(NX).reshape(GX, XL)[ORDER].reshape(NX), TRIPLES, NX)
     return np.concatenate(split(np.cos(a)) + split(np.sin(a)), 1)
 
 
@@ -219,11 +221,15 @@
     return 2 * lax.axis_index("chip") + lax.axis_index("core")
 
 
+def first_of(member):
+    return 32 * (member % 2) + member // 2
+
+
 def k2(in_ref, spec_ref, ty_ref, out_ref, scratch):
     for x, v in enumerate(y_transform(in_ref[...].astype(F32), ty_ref, 16)):
         parts = [v[0:16], v[16:32], v[32:48], jnp.zeros((16, LANES), F32)]
         for b, part in enumerate(exchange(parts, 32)):
-            scratch[pl.ds(16 * b + x, 16, stride=64), :] = part
+            scratch[pl.ds(16 * first_of(b) + x, 16, stride=32), :] = part
     quarter = place() % 4
     row = lax.broadcasted_iota(jnp.int32, (MY, OWNED), 0)
     mode = ky_of(lax.broadcasted_iota(jnp.int32, (MY, OWNED), 1), quarter)
@@ -233,7 +239,7 @@
         for k in range(4):
             for i in range(3):
                 part = moved[16 * i : 16 * i + 16, LANES * k : LANES * k + LANES]
-                scratch[pl.ds(16 * b + 4 + 4 * i + k, 16, stride=64), :] = part
+                scratch[pl.ds(16 * first_of(b) + 4 + 4 * i + k, 16, stride=32), :] = part
     out_ref[...] = scratch[...].astype(BF)
 
 
@@ -271,7 +277,7 @@
     def weights(i, k):
         at = 4 + 4 * i + k
         return jnp.concatenate(
-            [scratch[pl.ds(16 * source[r] + at, 16, stride=64), :] for r in range(3)], 0
+            [scratch[pl.ds(16 * first_of(source[r]) + at, 16, stride=32), :] for r in range(3)], 0
         )
 
     sums = []
@@ -295,7 +301,7 @@
     moved = jnp.concatenate(moved, 0).astype(BF)
     row = lax.broadcasted_iota(jnp.int32, (NX, 3 * MX), 0)
     col = lax.broadcasted_iota(jnp.int32, (NX, 3 * MX), 1)
-    owner = row // 4
+    owner = 2 * (row // 4 % 32) + row // 128
     quarter = owner % 4
     back_one = jnp.where(quarter == 1, jnp.where(a >= 12, 1, 0), 0)
     back_one += jnp.where(quarter == 2, jnp.where(a >= 8, 1, 0), 0)
@@ -310,7 +316,7 @@
 def k4(in_ref, ty_ref, out_ref, fwd_ref, scratch):
     scratch[...] = in_ref[...].astype(F32)
     for x in range(XL):
-        parts = [scratch[pl.ds(4 * b + x, 16, stride=16), :] for b in range(KZL)]
+        parts = [scratch[pl.ds(4 * first_of(b) + x, 16, stride=8), :] for b in range(KZL)]
         parts = exchange(parts, 32)
         if x < 3:
             fwd_ref[16 * x : 16 * x + 16, :] = parts[3]
@@ -479,7 +485,7 @@
         jnp.asarray(y_forward_table(TRIPLES)),
         scratch=[pltpu.VMEM((GX * 16, LANES), F32)],
     )
-    got = swap(sent.reshape(GX, 16, LANES), GXS).reshape(GX * 16, LANES)
+    got = swap(sent.reshape(GX, 16, LANES), CORE_FIRST).reshape(GX * 16, LANES)
     sent = call(
         k3,
         jax.ShapeDtypeStruct((NX, LANES), BF),
@@ -489,7 +495,7 @@
         jnp.asarray(x_inverse_table()),
         scratch=[pltpu.VMEM((GX * 16, LANES), F32)],
     )
-    back = swap(sent.reshape(GX, XL, LANES), GXS).reshape(NX, LANES)
+    back = swap(sent.reshape(GX, XL, LANES), CORE_FIRST).reshape(NX, LANES)
     waves, fwd = call(
         k4,
         (zshape, jax.ShapeDtypeStruct((MY, LANES), F32)),

time: 114 us -> 113 us (level)
  no operation moved by 1% of the time
where the time goes in v6:
time: 113 us
  blocking collectives  102 us (90%)
  Pallas kernels  10.3 us (9%)
    all_to_all x6, blocking collectives, swap(): return lax.all_to_all(value, axis, split_axis=0, concat_axis=0, tiled=True)  102 us
    pallas_call x7, Pallas kernels, call(): pl.pallas_call(body, out_shape=out, in_specs=specs, out_specs=jax.tree.ma...  10.3 us

profile of v6, /device:TPU:1, one launch (start us, length us, event | category | flops | bytes accessed | tf_op | source)
XLA Modules:
  0.0 113.0 jit_solution(1527517134232739888)
XLA Ops:
  0.0 0.0 copy-start.12
  0.0 2.6 %shard_map.172 = (bf16[8,96,128]{2,1,0:T(8,128)(2,1)S(1)}, bf16[256,256]{1,0:T(8,128)(2,1)S(1)}) custom-call(bf16[16,96,512]{2,1,0:T(8,128)(2,1)} %bitcast.19, bf16[1024,128]{1,0:T(8,128)(2,1)} %constant.26.clone.w_ref, bf16[16,16]{1,0:T(8,128)(2,1)} %pw_ref.1), custom_call_target="tpu_custom_call" | custom-call | tf_op jit(solution)/shard_map/pallas_call | solution.py:443
  2.6 0.0 copy-start.4
  2.6 0.0 copy-start.10
  2.7 16.3 %all_to_all.30.in_ref = bf16[8,96,128]{2,1,0:T(8,128)(2,1)S(1)} all-to-all(bf16[8,96,128]{2,1,0:T(8,128)(2,1)S(1)} %get-tuple-element.9), channel_id=1, replica_groups=mesh['chip'=32,'core'=2,'gy'=8] {'gy'}, dimensions={0} | all-to-all | bytes 393216 | tf_op jit(solution)/shard_map/all_to_all | solution.py:454
  19.0 0.0 copy-start.5
  19.0 0.0 copy-start.6
  19.0 0.7 shard_map.173
  19.7 28.2 %all_to_all.31 = bf16[64,16,128]{2,1,0:T(8,128)(2,1)S(1)} all-to-all(bf16[64,16,128]{2,1,0:T(8,128)(2,1)S(1)} %bitcast.26), channel_id=1, replica_groups=mesh['chip'=32,'core'=2,'gy'=8] {'core','chip'}, dimensions={0} | all-to-all | bytes 524288 | tf_op jit(solution)/shard_map/all_to_all | solution.py:454
  47.9 1.0 shard_map.174
  48.9 15.1 %all_to_all.32 = bf16[64,4,128]{2,1,0:T(4,128)(2,1)S(1)} all-to-all(bf16[64,4,128]{2,1,0:T(4,128)(2,1)S(1)} %bitcast.30), channel_id=1, replica_groups=mesh['chip'=32,'core'=2,'gy'=8] {'core','chip'}, dimensions={0} | all-to-all | bytes 131072 | tf_op jit(solution)/shard_map/all_to_all | solution.py:454
  64.1 0.5 shard_map.175
  64.6 13.3 %all_to_all.33.waves_ref = bf16[8,96,128]{2,1,0:T(8,128)(2,1)S(1)} all-to-all(bf16[8,96,128]{2,1,0:T(8,128)(2,1)S(1)} %get-tuple-element.10), channel_id=1, replica_groups=mesh['chip'=32,'core'=2,'gy'=8] {'gy'}, dimensions={0} | all-to-all | bytes 393216 | tf_op jit(solution)/shard_map/all_to_all | solution.py:454
  77.9 0.0 copy-start.7
  77.9 0.0 copy-start.8
  77.9 0.0 copy-start.13
  77.9 0.0 copy-start.14
  78.0 2.8 %shard_map.176 = bf16[16,48,128]{2,1,0:T(8,128)(2,1)S(1)} custom-call(bf16[8,96,128]{2,1,0:T(8,128)(2,1)S(1)} %all_to_all.33.waves_ref, bf16[16,96,512]{2,1,0:T(8,128)(2,1)S(1)} %bitcast.20, bf16[16,96,512]{2,1,0:T(8,128)(2,1)S(1)} %bitcast.23, bf16[256,256]{1,0:T(8,128)(2,1)S(1)} %get-tuple-element.11.kron, bf16[1024,128]{1,0:T(8,128)(2,1)S(1)} %copy-done.6, ...), custom_call_target="tpu_custom_call" | custom-call | tf_op jit(solution)/shard_map/pallas_call | solution.py:443
  80.7 0.0 copy-start.3
  80.7 0.0 copy-start.15
  80.8 11.4 %all_to_all.34.in_ref = bf16[16,48,128]{2,1,0:T(8,128)(2,1)S(1)} all-to-all(bf16[16,48,128]{2,1,0:T(8,128)(2,1)S(1)} %shard_map.176), channel_id=1, replica_groups=mesh['chip'=32,'core'=2,'gy'=8] {'core','gy'}, dimensions={0} | all-to-all | bytes 393216 | tf_op jit(solution)/shard_map/all_to_all | solution.py:454
  92.2 1.0 shard_map.177
  93.2 18.2 %all_to_all.35 = bf16[64,9,2,128]{3,2,1,0:T(2,128)(2,1)S(1)} all-to-all(bf16[64,9,2,128]{3,2,1,0:T(2,128)(2,1)S(1)} %bitcast.24), channel_id=1, replica_groups=mesh['chip'=32,'core'=2,'gy'=8] {'chip','core'}, dimensions={0} | all-to-all | bytes 589824 | tf_op jit(solution)/shard_map/all_to_all | solution.py:454
  111.4 1.6 %shard_map.178 = f32[2,16,64,36]{3,2,1,0:T(8,128)} custom-call(bf16[1152,128]{1,0:T(8,128)(2,1)S(1)} %bitcast.25, f32[48,128]{1,0:T(8,128)S(1)} %get-tuple-element.12.fwd_ref, bf16[128,128]{1,0:T(8,128)(2,1)S(1)} %copy-done.15, f32[2,16,64,36]{3,2,1,0:T(8,128)S(1)} %bitcast.22, f32[2,16,64,36]{3,2,1,0:T(8,128)S(1)} %bitcast.27), custom_call_target="tpu_custom_call" | custom-call | tf_op jit(solution)/shard_map/pallas_call | solution.py:443
  (21 shorter events, 0.0 us)
Async XLA Ops:
  0.0 19.0 %copy-start.11 = (bf16[192,192]{1,0:T(8,128)(2,1)S(1)}, bf16[192,192]{1,0:T(8,128)(2,1)}, u32[]{:S(2)}) copy-start(bf16[192,192]{1,0:T(8,128)(2,1)} %constant.29.clone.ty_ref) | copy-start | bytes 221188
  0.0 19.0 %copy-start.1 = (f32[36,2,16,16,4]{0,4,3,2,1:T(4,128)S(1)}, f32[36,2,16,16,4]{0,4,3,2,1:T(4,128)}, u32[]{:S(2)}) copy-start(f32[36,2,16,16,4]{0,4,3,2,1:T(4,128)} %param.20) | copy-start | bytes 884740
  0.0 47.9 %copy-start.9 = (bf16[256,192]{1,0:T(8,128)(2,1)S(1)}, bf16[256,192]{1,0:T(8,128)(2,1)}, u32[]{:S(2)}) copy-start(bf16[256,192]{1,0:T(8,128)(2,1)} %constant.32.clone.tinv_ref) | copy-start | bytes 294916
  0.0 64.1 %copy-start.12 = (bf16[192,192]{1,0:T(8,128)(2,1)S(1)}, bf16[192,192]{1,0:T(8,128)(2,1)}, u32[]{:S(2)}) copy-start(bf16[192,192]{1,0:T(8,128)(2,1)} %constant.33.clone.ty_ref) | copy-start | bytes 221188
  2.6 45.3 %copy-start.4 = (bf16[128,1536]{1,0:T(8,128)(2,1)S(1)}, bf16[128,1536]{1,0:T(8,128)(2,1)}, u32[]{:S(2)}) copy-start(bf16[128,1536]{1,0:T(8,128)(2,1)} %constant.31.clone.e_ref) | copy-start | bytes 1179652
  2.6 45.3 %copy-start.10 = (bf16[192,256]{1,0:T(8,128)(2,1)S(1)}, bf16[192,256]{1,0:T(8,128)(2,1)}, u32[]{:S(2)}) copy-start(bf16[192,256]{1,0:T(8,128)(2,1)} %constant.30.clone.tx_ref) | copy-start | bytes 294916
  19.0 58.9 %copy-start = (bf16[16,4,24,512]{3,2,1,0:T(8,128)(2,1)S(1)}, bf16[16,4,24,512]{3,2,1,0:T(8,128)(2,1)}, u32[]{:S(2)}) copy-start(bf16[16,4,24,512]{3,2,1,0:T(8,128)(2,1)} %param.18) | copy-start | bytes 4718596
  19.0 58.9 %copy-start.2 = (bf16[16,4,24,512]{3,2,1,0:T(8,128)(2,1)S(1)}, bf16[16,4,24,512]{3,2,1,0:T(8,128)(2,1)}, u32[]{:S(2)}) copy-start(bf16[16,4,24,512]{3,2,1,0:T(8,128)(2,1)} %param.22) | copy-start | bytes 4718596
  19.0 58.9 %copy-start.5 = (bf16[128,1024]{1,0:T(8,128)(2,1)S(1)}, bf16[128,1024]{1,0:T(8,128)(2,1)}, u32[]{:S(2)}) copy-start(bf16[128,1024]{1,0:T(8,128)(2,1)} %constant.28.clone.zt_ref) | copy-start | bytes 786436
  19.0 58.9 %copy-start.6 = (bf16[1024,128]{1,0:T(8,128)(2,1)S(1)}, bf16[1024,128]{1,0:T(8,128)(2,1)}, u32[]{:S(2)}) copy-start(bf16[1024,128]{1,0:T(8,128)(2,1)} %constant.27.clone.w_ref) | copy-start | bytes 786436
  77.9 14.2 %copy-start.7 = (f32[384,128]{1,0:T(8,128)S(1)}, f32[384,128]{1,0:T(8,128)}, u32[]{:S(2)}) copy-start(f32[384,128]{1,0:T(8,128)} %constant.36.clone.turn_ref) | copy-start | bytes 589828
  77.9 14.2 %copy-start.8 = (f32[384,128]{1,0:T(8,128)S(1)}, f32[384,128]{1,0:T(8,128)}, u32[]{:S(2)}) copy-start(f32[384,128]{1,0:T(8,128)} %constant.35.clone.near_ref) | copy-start | bytes 589828
  77.9 14.2 %copy-start.13 = (bf16[192,192]{1,0:T(8,128)(2,1)S(1)}, bf16[192,192]{1,0:T(8,128)(2,1)}, u32[]{:S(2)}) copy-start(bf16[192,192]{1,0:T(8,128)(2,1)} %constant.34.clone.ty_ref) | copy-start | bytes 221188
  77.9 14.2 %copy-start.14 = (bf16[96,256]{1,0:T(8,128)(2,1)S(1)}, bf16[96,256]{1,0:T(8,128)(2,1)}, u32[]{:S(2)}) copy-start(bf16[96,256]{1,0:T(8,128)(2,1)} %constant.37.clone.chip_ref) | copy-start | bytes 147460
  80.7 30.6 %copy-start.3 = (f32[36,2,16,16,4]{0,4,3,2,1:T(4,128)S(1)}, f32[36,2,16,16,4]{0,4,3,2,1:T(4,128)}, u32[]{:S(2)}) copy-start(f32[36,2,16,16,4]{0,4,3,2,1:T(4,128)} %param.21) | copy-start | bytes 884740
  80.7 30.6 %copy-start.15 = (bf16[128,128]{1,0:T(8,128)(2,1)S(1)}, bf16[128,128]{1,0:T(8,128)(2,1)}, u32[]{:S(2)}) copy-start(bf16[128,128]{1,0:T(8,128)(2,1)} %constant.38.clone.reorder_ref) | copy-start | bytes 98308

commit v7 on v6

--- a/solution.py
+++ b/solution.py
@@ -178,8 +178,6 @@
 
 
 def k1(field_ref, w_ref, pw_ref, out_ref, kron_ref, x_ref, t_ref, p_ref, sems):
-    small = pltpu.make_async_copy(pw_ref, p_ref, sems.at[9])
-    small.start()
     table = pltpu.make_async_copy(w_ref, t_ref, sems.at[8])
     table.start()
     copies = []
@@ -188,6 +186,8 @@
             part = pl.ds(8 * h + 2 * n, 2)
             copies.append(pltpu.make_async_copy(field_ref.at[part], x_ref.at[part], sems.at[2 * n + h]))
             copies[-1].start()
+    small = pltpu.make_async_copy(pw_ref, p_ref, sems.at[9])
+    small.start()
     small.wait()
     kron_ref[...] = expand_pointwise(p_ref[...])
     table.wait()

time: 113 us -> 114 us (level)
  no operation moved by 1% of the time
where the time goes in v7:
time: 114 us; the launch traced here: 113 us
  blocking collectives  102 us (89%)
  Pallas kernels  10.8 us (9%)
    all_to_all x6, blocking collectives, swap(): return lax.all_to_all(value, axis, split_axis=0, concat_axis=0, tiled=True)  102 us
    pallas_call x7, Pallas kernels, call(): pl.pallas_call(body, out_shape=out, in_specs=specs, out_specs=jax.tree.ma...  10.8 us

profile of v7, /device:TPU:1, one launch (start us, length us, event | category | flops | bytes accessed | tf_op | source)
XLA Modules:
  0.0 113.5 jit_solution(15719121888451652930)
XLA Ops:
  0.0 0.0 copy-start.12
  0.0 3.1 %shard_map.172 = (bf16[8,96,128]{2,1,0:T(8,128)(2,1)S(1)}, bf16[256,256]{1,0:T(8,128)(2,1)S(1)}) custom-call(bf16[16,96,512]{2,1,0:T(8,128)(2,1)} %bitcast.19, bf16[1024,128]{1,0:T(8,128)(2,1)} %constant.26.clone.w_ref, bf16[16,16]{1,0:T(8,128)(2,1)} %pw_ref.1), custom_call_target="tpu_custom_call" | custom-call | tf_op jit(solution)/shard_map/pallas_call | solution.py:443
  3.1 0.0 copy-start.4
  3.1 0.0 copy-start.10
  3.2 16.3 %all_to_all.30.in_ref = bf16[8,96,128]{2,1,0:T(8,128)(2,1)S(1)} all-to-all(bf16[8,96,128]{2,1,0:T(8,128)(2,1)S(1)} %get-tuple-element.9), channel_id=1, replica_groups=mesh['chip'=32,'core'=2,'gy'=8] {'gy'}, dimensions={0} | all-to-all | bytes 393216 | tf_op jit(solution)/shard_map/all_to_all | solution.py:454
  19.5 0.0 copy-start.5
  19.5 0.0 copy-start.6
  19.5 0.7 shard_map.173
  20.2 28.2 %all_to_all.31 = bf16[64,16,128]{2,1,0:T(8,128)(2,1)S(1)} all-to-all(bf16[64,16,128]{2,1,0:T(8,128)(2,1)S(1)} %bitcast.26), channel_id=1, replica_groups=mesh['chip'=32,'core'=2,'gy'=8] {'core','chip'}, dimensions={0} | all-to-all | bytes 524288 | tf_op jit(solution)/shard_map/all_to_all | solution.py:454
  48.4 1.0 shard_map.174
  49.4 15.1 %all_to_all.32 = bf16[64,4,128]{2,1,0:T(4,128)(2,1)S(1)} all-to-all(bf16[64,4,128]{2,1,0:T(4,128)(2,1)S(1)} %bitcast.30), channel_id=1, replica_groups=mesh['chip'=32,'core'=2,'gy'=8] {'core','chip'}, dimensions={0} | all-to-all | bytes 131072 | tf_op jit(solution)/shard_map/all_to_all | solution.py:454
  64.6 0.5 shard_map.175
  65.1 13.3 %all_to_all.33.waves_ref = bf16[8,96,128]{2,1,0:T(8,128)(2,1)S(1)} all-to-all(bf16[8,96,128]{2,1,0:T(8,128)(2,1)S(1)} %get-tuple-element.10), channel_id=1, replica_groups=mesh['chip'=32,'core'=2,'gy'=8] {'gy'}, dimensions={0} | all-to-all | bytes 393216 | tf_op jit(solution)/shard_map/all_to_all | solution.py:454
  78.4 0.0 copy-start.7
  78.4 0.0 copy-start.8
  78.4 0.0 copy-start.13
  78.5 0.0 copy-start.14
  78.5 2.8 %shard_map.176 = bf16[16,48,128]{2,1,0:T(8,128)(2,1)S(1)} custom-call(bf16[8,96,128]{2,1,0:T(8,128)(2,1)S(1)} %all_to_all.33.waves_ref, bf16[16,96,512]{2,1,0:T(8,128)(2,1)S(1)} %bitcast.20, bf16[16,96,512]{2,1,0:T(8,128)(2,1)S(1)} %bitcast.23, bf16[256,256]{1,0:T(8,128)(2,1)S(1)} %get-tuple-element.11.kron, bf16[1024,128]{1,0:T(8,128)(2,1)S(1)} %copy-done.6, ...), custom_call_target="tpu_custom_call" | custom-call | tf_op jit(solution)/shard_map/pallas_call | solution.py:443
  81.2 0.0 copy-start.3
  81.2 0.0 copy-start.15
  81.3 11.4 %all_to_all.34.in_ref = bf16[16,48,128]{2,1,0:T(8,128)(2,1)S(1)} all-to-all(bf16[16,48,128]{2,1,0:T(8,128)(2,1)S(1)} %shard_map.176), channel_id=1, replica_groups=mesh['chip'=32,'core'=2,'gy'=8] {'core','gy'}, dimensions={0} | all-to-all | bytes 393216 | tf_op jit(solution)/shard_map/all_to_all | solution.py:454
  92.7 1.0 shard_map.177
  93.7 18.2 %all_to_all.35 = bf16[64,9,2,128]{3,2,1,0:T(2,128)(2,1)S(1)} all-to-all(bf16[64,9,2,128]{3,2,1,0:T(2,128)(2,1)S(1)} %bitcast.24), channel_id=1, replica_groups=mesh['chip'=32,'core'=2,'gy'=8] {'chip','core'}, dimensions={0} | all-to-all | bytes 589824 | tf_op jit(solution)/shard_map/all_to_all | solution.py:454
  111.9 1.6 %shard_map.178 = f32[2,16,64,36]{3,2,1,0:T(8,128)} custom-call(bf16[1152,128]{1,0:T(8,128)(2,1)S(1)} %bitcast.25, f32[48,128]{1,0:T(8,128)S(1)} %get-tuple-element.12.fwd_ref, bf16[128,128]{1,0:T(8,128)(2,1)S(1)} %copy-done.15, f32[2,16,64,36]{3,2,1,0:T(8,128)S(1)} %bitcast.22, f32[2,16,64,36]{3,2,1,0:T(8,128)S(1)} %bitcast.27), custom_call_target="tpu_custom_call" | custom-call | tf_op jit(solution)/shard_map/pallas_call | solution.py:443
  (21 shorter events, 0.0 us)
Async XLA Ops:
  0.0 19.5 %copy-start.11 = (bf16[192,192]{1,0:T(8,128)(2,1)S(1)}, bf16[192,192]{1,0:T(8,128)(2,1)}, u32[]{:S(2)}) copy-start(bf16[192,192]{1,0:T(8,128)(2,1)} %constant.29.clone.ty_ref) | copy-start | bytes 221188
  0.0 19.5 %copy-start.1 = (f32[36,2,16,16,4]{0,4,3,2,1:T(4,128)S(1)}, f32[36,2,16,16,4]{0,4,3,2,1:T(4,128)}, u32[]{:S(2)}) copy-start(f32[36,2,16,16,4]{0,4,3,2,1:T(4,128)} %param.20) | copy-start | bytes 884740
  0.0 48.4 %copy-start.9 = (bf16[256,192]{1,0:T(8,128)(2,1)S(1)}, bf16[256,192]{1,0:T(8,128)(2,1)}, u32[]{:S(2)}) copy-start(bf16[256,192]{1,0:T(8,128)(2,1)} %constant.32.clone.tinv_ref) | copy-start | bytes 294916
  0.0 64.6 %copy-start.12 = (bf16[192,192]{1,0:T(8,128)(2,1)S(1)}, bf16[192,192]{1,0:T(8,128)(2,1)}, u32[]{:S(2)}) copy-start(bf16[192,192]{1,0:T(8,128)(2,1)} %constant.33.clone.ty_ref) | copy-start | bytes 221188
  3.1 45.3 %copy-start.4 = (bf16[128,1536]{1,0:T(8,128)(2,1)S(1)}, bf16[128,1536]{1,0:T(8,128)(2,1)}, u32[]{:S(2)}) copy-start(bf16[128,1536]{1,0:T(8,128)(2,1)} %constant.31.clone.e_ref) | copy-start | bytes 1179652
  3.1 45.3 %copy-start.10 = (bf16[192,256]{1,0:T(8,128)(2,1)S(1)}, bf16[192,256]{1,0:T(8,128)(2,1)}, u32[]{:S(2)}) copy-start(bf16[192,256]{1,0:T(8,128)(2,1)} %constant.30.clone.tx_ref) | copy-start | bytes 294916
  19.5 58.9 %copy-start = (bf16[16,4,24,512]{3,2,1,0:T(8,128)(2,1)S(1)}, bf16[16,4,24,512]{3,2,1,0:T(8,128)(2,1)}, u32[]{:S(2)}) copy-start(bf16[16,4,24,512]{3,2,1,0:T(8,128)(2,1)} %param.18) | copy-start | bytes 4718596
  19.5 58.9 %copy-start.2 = (bf16[16,4,24,512]{3,2,1,0:T(8,128)(2,1)S(1)}, bf16[16,4,24,512]{3,2,1,0:T(8,128)(2,1)}, u32[]{:S(2)}) copy-start(bf16[16,4,24,512]{3,2,1,0:T(8,128)(2,1)} %param.22) | copy-start | bytes 4718596
  19.5 58.9 %copy-start.5 = (bf16[128,1024]{1,0:T(8,128)(2,1)S(1)}, bf16[128,1024]{1,0:T(8,128)(2,1)}, u32[]{:S(2)}) copy-start(bf16[128,1024]{1,0:T(8,128)(2,1)} %constant.28.clone.zt_ref) | copy-start | bytes 786436
  19.5 58.9 %copy-start.6 = (bf16[1024,128]{1,0:T(8,128)(2,1)S(1)}, bf16[1024,128]{1,0:T(8,128)(2,1)}, u32[]{:S(2)}) copy-start(bf16[1024,128]{1,0:T(8,128)(2,1)} %constant.27.clone.w_ref) | copy-start | bytes 786436
  78.4 14.2 %copy-start.7 = (f32[384,128]{1,0:T(8,128)S(1)}, f32[384,128]{1,0:T(8,128)}, u32[]{:S(2)}) copy-start(f32[384,128]{1,0:T(8,128)} %constant.36.clone.turn_ref) | copy-start | bytes 589828
  78.4 14.2 %copy-start.8 = (f32[384,128]{1,0:T(8,128)S(1)}, f32[384,128]{1,0:T(8,128)}, u32[]{:S(2)}) copy-start(f32[384,128]{1,0:T(8,128)} %constant.35.clone.near_ref) | copy-start | bytes 589828
  78.4 14.2 %copy-start.13 = (bf16[192,192]{1,0:T(8,128)(2,1)S(1)}, bf16[192,192]{1,0:T(8,128)(2,1)}, u32[]{:S(2)}) copy-start(bf16[192,192]{1,0:T(8,128)(2,1)} %constant.34.clone.ty_ref) | copy-start | bytes 221188
  78.5 14.2 %copy-start.14 = (bf16[96,256]{1,0:T(8,128)(2,1)S(1)}, bf16[96,256]{1,0:T(8,128)(2,1)}, u32[]{:S(2)}) copy-start(bf16[96,256]{1,0:T(8,128)(2,1)} %constant.37.clone.chip_ref) | copy-start | bytes 147460
  81.2 30.6 %copy-start.3 = (f32[36,2,16,16,4]{0,4,3,2,1:T(4,128)S(1)}, f32[36,2,16,16,4]{0,4,3,2,1:T(4,128)}, u32[]{:S(2)}) copy-start(f32[36,2,16,16,4]{0,4,3,2,1:T(4,128)} %param.21) | copy-start | bytes 884740
  81.2 30.6 %copy-start.15 = (bf16[128,128]{1,0:T(8,128)(2,1)S(1)}, bf16[128,128]{1,0:T(8,128)(2,1)}, u32[]{:S(2)}) copy-start(bf16[128,128]{1,0:T(8,128)(2,1)} %constant.38.clone.reorder_ref) | copy-start | bytes 98308
